TPU v7x, 128 devices: a whole 4x4x4 slice. The times are simulated.
128 devices in a mesh: wide: 16 (over x_lo, y, core), narrow: 8 (over x_hi, z).
Axes of the slice: x: 4 (x_hi: 2, x_lo: 2; x = x_hi * 2 + x_lo), y: 4, z: 4, core: 2. Of those that a mesh axis runs over, the one named last changes fastest.
Arguments:
- tokens: bfloat16 [2, 4096, 2048], P(None, 'wide'), may hold values from -6 to 6
- cotangent: bfloat16 [2, 4096, 2048], P(None, 'wide'), may hold values from -6 to 6
- lengths: int32 [2], replicated, may hold values from 256 to 4096, as said below
- query_weight: bfloat16 [2048, 2048], P(None, 'narrow'), may hold values from -0.125 to 0.125
- keyval_weight: bfloat16 [2, 2048, 512], P(None, None, 'narrow'), may hold values from -0.125 to 0.125
- output_weight: bfloat16 [2048, 2048], P('narrow'), may hold values from -0.75 to 0.75
- gateup_weight: bfloat16 [2, 2048, 8192], P(None, None, 'narrow'), may hold values from -1 to 1
- down_weight: bfloat16 [8192, 2048], P('narrow'), may hold values from -0.0625 to 0.0625
- norm_gains: bfloat16 [2, 2048], replicated, may hold values from 0.25 to 3
- query_first: float32 [2048, 2048], P('wide', 'narrow'), may hold values from -9.1552734e-05 to 9.1552734e-05
- keyval_first: float32 [2, 2048, 512], P(None, 'wide', 'narrow'), may hold values from -9.1552734e-05 to 9.1552734e-05
- output_first: float32 [2048, 2048], P('narrow', 'wide'), may hold values from -9.1552734e-05 to 9.1552734e-05
- gateup_first: float32 [2, 2048, 8192], P(None, 'wide', 'narrow'), may hold values from -9.1552734e-05 to 9.1552734e-05
- down_first: float32 [8192, 2048], P('narrow', 'wide'), may hold values from -9.1552734e-05 to 9.1552734e-05
- gains_first: float32 [2, 2048], P(None, 'wide'), may hold values from -9.1552734e-05 to 9.1552734e-05
- query_second: float32 [2048, 2048], P('wide', 'narrow'), may hold values from 4.2748038e-10 to 6.905452e-09
- keyval_second: float32 [2, 2048, 512], P(None, 'wide', 'narrow'), may hold values from 4.2748038e-10 to 6.905452e-09
- output_second: float32 [2048, 2048], P('narrow', 'wide'), may hold values from 5.3435048e-11 to 8.631815e-10
- gateup_second: float32 [2, 2048, 8192], P(None, 'wide', 'narrow'), may hold values from 4.2748038e-10 to 6.905452e-09
- down_second: float32 [8192, 2048], P('narrow', 'wide'), may hold values from 4.2748038e-10 to 6.905452e-09
- gains_second: float32 [2, 2048], P(None, 'wide'), may hold values from 4.2748038e-10 to 6.905452e-09
Outputs:
- layer_out: bfloat16 [2, 4096, 2048], P(None, 'wide')
- input_grad: bfloat16 [2, 4096, 2048], P(None, 'wide')
- query_grad: float32 [2048, 2048], P('wide', 'narrow')
- keyval_grad: float32 [2, 2048, 512], P(None, 'wide', 'narrow')
- output_grad: float32 [2048, 2048], P('narrow', 'wide')
- gateup_grad: float32 [2, 2048, 8192], P(None, 'wide', 'narrow')
- down_grad: float32 [8192, 2048], P('narrow', 'wide')
- gains_grad: float32 [2, 2048], P(None, 'wide')
- grad_norm: float32 [], replicated
- query_momentum: float32 [2048, 2048], P('wide', 'narrow')
- keyval_momentum: float32 [2, 2048, 512], P(None, 'wide', 'narrow')
- output_momentum: float32 [2048, 2048], P('narrow', 'wide')
- gateup_momentum: float32 [2, 2048, 8192], P(None, 'wide', 'narrow')
- down_momentum: float32 [8192, 2048], P('narrow', 'wide')
- gains_momentum: float32 [2, 2048], P(None, 'wide')
- query_variance: float32 [2048, 2048], P('wide', 'narrow')
- keyval_variance: float32 [2, 2048, 512], P(None, 'wide', 'narrow')
- output_variance: float32 [2048, 2048], P('narrow', 'wide')
- gateup_variance: float32 [2, 2048, 8192], P(None, 'wide', 'narrow')
- down_variance: float32 [8192, 2048], P('narrow', 'wide')
- gains_variance: float32 [2, 2048], P(None, 'wide')
- query_updated: float32 [2048, 2048], P('wide', 'narrow')
- keyval_updated: float32 [2, 2048, 512], P(None, 'wide', 'narrow')
- output_updated: float32 [2048, 2048], P('narrow', 'wide')
- gateup_updated: float32 [2, 2048, 8192], P(None, 'wide', 'narrow')
- down_updated: float32 [8192, 2048], P('narrow', 'wide')
- gains_updated: float32 [2, 2048], P(None, 'wide')
Inputs may be any that keep to these rules, and one draw needn't show every extreme that they name: `lengths`: in every draw one bucket, which one drawn from the seed, holds a sequence of all 4096 positions.
All inputs are finite; a program needn't handle non-finite values.
Results may differ from a plain program's by a relative error of at most 0.04.
Values may be sent and summed in bfloat16 or wider, within the bound.
A program may use at most 192 MiB of HBM per device.

v0:
```python
import math

import jax
import jax.numpy as jnp
from jax import lax
from jax.sharding import PartitionSpec as P

HD = 64
STEP = 10


norm_eps = 1e-05
rope_theta = 500000.0
rope_factor = 32.0
rope_low = 1.0
rope_high = 4.0
rope_context = 8192.0
clip_limit = 1.0
beta_first = 0.9
beta_second = 0.95
adam_eps = 1e-08
learn_rate = 0.09
gain_rate = 1.2
decay_rate = 0.1
masked_score = -1e30


def sent_to_all(x, axis):
    peers = lax.axis_size(axis)
    return lax.all_to_all(jnp.broadcast_to(x[None], (peers, *x.shape)), axis, 0, 0, tiled=True)


def in_order(blocks, dim):
    shape = list(blocks.shape[1:])
    shape[dim] *= blocks.shape[0]
    return jnp.moveaxis(blocks, 0, dim).reshape(shape)


def gather_directly(x, axis, dim):
    blocks = sent_to_all(x, axis)
    return in_order(blocks, dim)


def cut_along(x, dim, peers):
    before, after = (x.shape[:dim], x.shape[dim + 1 :])
    return jnp.moveaxis(x.reshape(*before, peers, -1, *after), dim, 0)


def sent_and_summed(x, axis, dim):
    peers = lax.axis_size(axis)
    blocks = lax.all_to_all(cut_along(x, dim, peers), axis, 0, 0, tiled=True)
    return jnp.sum(blocks.astype(jnp.float32), axis=0)


def rope_tables(positions, head_width):
    half_width = head_width // 2
    exponent = jnp.arange(half_width, dtype=jnp.float32) * (2.0 / head_width)
    base_freq = jnp.power(jnp.float32(rope_theta), -exponent)
    wavelen = 2.0 * math.pi / base_freq
    smooth = (rope_context / wavelen - rope_low) / (rope_high - rope_low)
    blended = (1.0 - smooth) * base_freq / rope_factor + smooth * base_freq
    scaled = jnp.where(
        wavelen < rope_context / rope_high,
        base_freq,
        jnp.where(wavelen > rope_context / rope_low, base_freq / rope_factor, blended),
    )
    angles = positions.astype(jnp.float32)[:, None] * scaled[None, :]
    return (jnp.cos(angles), jnp.sin(angles))


def rotate(values, cosine, sine_table):
    half_width = values.shape[-1] // 2
    front_half = values[..., :half_width]
    back_half = values[..., half_width:]
    cosine = cosine[:, None, :]
    sine_table = sine_table[:, None, :]
    return jnp.concatenate(
        [
            front_half * cosine - back_half * sine_table,
            back_half * cosine + front_half * sine_table,
        ],
        axis=-1,
    )


def rotate_back(gradient, cosine, sine_table):
    half_width = gradient.shape[-1] // 2
    front_half = gradient[..., :half_width]
    back_half = gradient[..., half_width:]
    cosine = cosine[:, None, :]
    sine_table = sine_table[:, None, :]
    return jnp.concatenate(
        [
            front_half * cosine + back_half * sine_table,
            back_half * cosine - front_half * sine_table,
        ],
        axis=-1,
    )


def normalize(values):
    inverse = lax.rsqrt(jnp.mean(values * values, axis=-1, keepdims=True) + norm_eps)
    return (values * inverse, inverse)


def norm_back(grad_scaled, scaled, inverse):
    return inverse * (grad_scaled - scaled * jnp.mean(grad_scaled * scaled, axis=-1, keepdims=True))


def to_groups(values, groups):
    bucket_count, row_count, head_count, head_width = values.shape
    grouped = values.reshape(bucket_count, row_count, groups, head_count // groups, head_width)
    grouped = grouped.transpose(0, 2, 3, 1, 4)
    return grouped.reshape(bucket_count, groups, head_count // groups * row_count, head_width)


def from_groups(values, row_count):
    bucket_count, groups, merged, head_width = values.shape
    per_group = merged // row_count
    spread = values.reshape(bucket_count, groups, per_group, row_count, head_width)
    return spread.transpose(0, 3, 1, 2, 4).reshape(
        bucket_count, row_count, groups * per_group, head_width
    )


def adam_update(weight, gradient, old_first, old_second, step_rate, decay_factor):
    momentum = beta_first * old_first + (1.0 - beta_first) * gradient
    variance = beta_second * old_second + (1.0 - beta_second) * gradient * gradient
    corrected = momentum / (1.0 - beta_first**STEP)
    second_hat = variance / (1.0 - beta_second**STEP)
    updated = weight * (1.0 - step_rate * decay_factor) - step_rate * corrected / (
        jnp.sqrt(second_hat) + adam_eps
    )
    return (updated, momentum, variance)


def row_sum(values):
    return lax.psum_scatter(
        values.astype(jnp.bfloat16), "narrow", scatter_dimension=0, tiled=True
    ).astype(jnp.float32)


def row_collect(values):
    return gather_directly(values, "narrow", 0)


def gain_total(values):
    return lax.psum(values, "narrow")


def shards(
    tokens,
    cotangent,
    lengths,
    query_weight,
    keyval_weight,
    output_weight,
    gateup_weight,
    down_weight,
    norm_gains,
    query_first,
    keyval_first,
    output_first,
    gateup_first,
    down_first,
    gains_first,
    query_second,
    keyval_second,
    output_second,
    gateup_second,
    down_second,
    gains_second,
):
    bucket_count, row_count, model_width = tokens.shape
    wide_count = lax.axis_size("wide")
    narrow_count = lax.axis_size("narrow")
    wide_rank = lax.axis_index("wide")
    narrow_rank = lax.axis_index("narrow")
    head_count = query_weight.shape[1] // HD
    group_count = keyval_weight.shape[2] // HD
    pair_width = group_count * HD
    token_count = bucket_count * row_count
    share_rows = token_count // narrow_count
    bucket_len = row_count * wide_count
    score_scale = HD ** (-0.5)
    positions = wide_rank * row_count + jnp.arange(row_count, dtype=jnp.int32)
    last_position = wide_rank * row_count + row_count - 1
    cosine, sine_table = rope_tables(positions, HD)
    gains = norm_gains.astype(jnp.float32)
    inputs = tokens.astype(jnp.float32).reshape(token_count, model_width)

    def rows_of(values):
        return lax.dynamic_slice_in_dim(values, narrow_rank * share_rows, share_rows, 0)

    scaled_one, inverse_one = normalize(inputs)
    normed_one = (scaled_one * gains[0]).astype(jnp.bfloat16)
    query_pre = jnp.dot(normed_one, query_weight, preferred_element_type=jnp.float32)
    keyval_pre = jnp.einsum(
        "nd,cde->cne", normed_one, keyval_weight, preferred_element_type=jnp.float32
    )
    query_heads = rotate(
        query_pre.reshape(bucket_count, row_count, head_count, HD), cosine, sine_table
    ).astype(jnp.bfloat16)
    key_heads = rotate(
        keyval_pre[0].reshape(bucket_count, row_count, group_count, HD), cosine, sine_table
    )
    key_flat = key_heads.reshape(bucket_count, row_count, pair_width)
    value_flat = keyval_pre[1].reshape(bucket_count, row_count, pair_width)
    local_pairs = jnp.concatenate([key_flat, value_flat], axis=-1).astype(jnp.bfloat16)
    all_pairs = lax.all_gather(local_pairs, "wide", axis=1, tiled=True)
    key_full = (
        all_pairs[..., :pair_width]
        .reshape(bucket_count, bucket_len, group_count, HD)
        .transpose(0, 2, 1, 3)
    )
    value_full = (
        all_pairs[..., pair_width:]
        .reshape(bucket_count, bucket_len, group_count, HD)
        .transpose(0, 2, 1, 3)
    )
    query_rows = to_groups(query_heads, group_count)
    group_rows = query_rows.shape[2]
    query_place = jnp.tile(positions, group_rows // row_count)
    key_block = math.gcd(bucket_len, 512)
    block_count = bucket_len // key_block

    def block_scores(key_rows, offset):
        raw_scores = (
            jnp.einsum("bkrh,bkmh->bkrm", query_rows, key_rows, preferred_element_type=jnp.float32)
            * score_scale
        )
        key_place = offset + jnp.arange(key_block, dtype=jnp.int32)
        causal = key_place[None, :] <= query_place[:, None]
        inside = key_place[None, :] < lengths[:, None]
        allowed = causal[None, None, :, :] & inside[:, None, None, :]
        return jnp.where(allowed, raw_scores, masked_score)

    def forward_block(running, block_index):
        offset = block_index * key_block
        key_rows = lax.dynamic_slice_in_dim(key_full, offset, key_block, 2)
        value_rows = lax.dynamic_slice_in_dim(value_full, offset, key_block, 2)

        def forward_attend(running):
            row_best, row_total, weighted = running
            scores = block_scores(key_rows, offset)
            new_best = jnp.maximum(row_best, jnp.max(scores, axis=-1))
            rescale = jnp.exp(row_best - new_best)
            weights = jnp.exp(scores - new_best[..., None])
            row_total = row_total * rescale + jnp.sum(weights, axis=-1)
            weighted = weighted * rescale[..., None] + jnp.einsum(
                "bkrm,bkmh->bkrh",
                weights.astype(jnp.bfloat16),
                value_rows,
                preferred_element_type=jnp.float32,
            )
            return (new_best, row_total, weighted)

        return (lax.cond(offset <= last_position, forward_attend, lambda held: held, running), None)

    initial = (
        jnp.full((bucket_count, group_count, group_rows), masked_score, jnp.float32),
        jnp.zeros((bucket_count, group_count, group_rows), jnp.float32),
        jnp.zeros((bucket_count, group_count, group_rows, HD), jnp.float32),
    )
    (row_best, row_total, weighted), _ = lax.scan(forward_block, initial, jnp.arange(block_count))
    log_total = row_best + jnp.log(row_total)
    attended = weighted / row_total[..., None]
    attended_low = (
        from_groups(attended, row_count).reshape(token_count, head_count * HD).astype(jnp.bfloat16)
    )
    attention_part = jnp.dot(attended_low, output_weight, preferred_element_type=jnp.float32)
    hidden = rows_of(inputs) + row_sum(attention_part)
    scaled_two, inverse_two = normalize(hidden)
    normed_two = row_collect((scaled_two * gains[1]).astype(jnp.bfloat16))
    gate_up = jnp.einsum(
        "nd,cdf->cnf", normed_two, gateup_weight, preferred_element_type=jnp.float32
    )
    gate_values = gate_up[0]
    up_values = gate_up[1]
    sigmoid_gate = jax.nn.sigmoid(gate_values)
    activated = gate_values * sigmoid_gate
    mixed = (activated * up_values).astype(jnp.bfloat16)
    feedforward_part = jnp.dot(mixed, down_weight, preferred_element_type=jnp.float32)
    result_rows = row_collect((hidden + row_sum(feedforward_part)).astype(jnp.bfloat16))
    layer_out = result_rows.reshape(bucket_count, row_count, model_width)
    live_mask = (positions[None, :] < lengths[:, None]).astype(jnp.float32)
    grad_result = (cotangent.astype(jnp.float32) * live_mask[:, :, None]).reshape(
        token_count, model_width
    )
    grad_low = grad_result.astype(jnp.bfloat16)
    down_grad = jnp.einsum("nf,nd->fd", mixed, grad_low, preferred_element_type=jnp.float32)
    grad_mixed = jnp.einsum("nd,fd->nf", grad_low, down_weight, preferred_element_type=jnp.float32)
    grad_gate = grad_mixed * up_values * sigmoid_gate * (1.0 + gate_values * (1.0 - sigmoid_gate))
    grad_up = grad_mixed * activated
    grad_gateup = jnp.stack([grad_gate, grad_up]).astype(jnp.bfloat16)
    gateup_grad = jnp.einsum(
        "nd,cnf->cdf", normed_two, grad_gateup, preferred_element_type=jnp.float32
    )
    normed_two_part = jnp.einsum(
        "cnf,cdf->nd", grad_gateup, gateup_weight, preferred_element_type=jnp.float32
    )
    grad_normed_two = row_sum(normed_two_part)
    gain_two_grad = gain_total(jnp.sum(grad_normed_two * scaled_two, axis=0))
    grad_hidden = rows_of(grad_result) + norm_back(
        grad_normed_two * gains[1], scaled_two, inverse_two
    )
    grad_branch = row_collect(grad_hidden.astype(jnp.bfloat16))
    output_grad = jnp.einsum(
        "ne,nd->ed", attended_low, grad_branch, preferred_element_type=jnp.float32
    )
    down_sum, gateup_sum, gain_two_sum, output_sum = (
        lax.psum_scatter(
            down_grad.astype(jnp.bfloat16), "wide", scatter_dimension=1, tiled=True
        ).astype(jnp.float32),
        lax.psum_scatter(
            gateup_grad.astype(jnp.bfloat16), "wide", scatter_dimension=1, tiled=True
        ).astype(jnp.float32),
        lax.psum_scatter(
            gain_two_grad.astype(jnp.bfloat16), "wide", scatter_dimension=0, tiled=True
        ).astype(jnp.float32),
        lax.psum_scatter(
            output_grad.astype(jnp.bfloat16), "wide", scatter_dimension=1, tiled=True
        ).astype(jnp.float32),
    )
    grad_heads = jnp.einsum(
        "nd,ed->ne", grad_branch, output_weight, preferred_element_type=jnp.float32
    ).astype(jnp.bfloat16)
    grad_rows = to_groups(grad_heads.reshape(bucket_count, row_count, head_count, HD), group_count)
    row_delta = jnp.sum(grad_rows.astype(jnp.float32) * attended, axis=-1)

    def backward_block(grad_query, block_index):
        offset = block_index * key_block
        key_rows = lax.dynamic_slice_in_dim(key_full, offset, key_block, 2)
        value_rows = lax.dynamic_slice_in_dim(value_full, offset, key_block, 2)

        def backward_attend(grad_query):
            scores = block_scores(key_rows, offset)
            probabilities = jnp.exp(scores - log_total[..., None])
            grad_probs = jnp.einsum(
                "bkrh,bkmh->bkrm", grad_rows, value_rows, preferred_element_type=jnp.float32
            )
            grad_scores = (probabilities * (grad_probs - row_delta[..., None])).astype(jnp.bfloat16)
            grad_query = (
                grad_query
                + jnp.einsum(
                    "bkrm,bkmh->bkrh", grad_scores, key_rows, preferred_element_type=jnp.float32
                )
                * score_scale
            )
            grad_key = (
                jnp.einsum(
                    "bkrm,bkrh->bkmh", grad_scores, query_rows, preferred_element_type=jnp.float32
                )
                * score_scale
            )
            grad_value = jnp.einsum(
                "bkrm,bkrh->bkmh",
                probabilities.astype(jnp.bfloat16),
                grad_rows,
                preferred_element_type=jnp.float32,
            )
            return (grad_query, jnp.concatenate([grad_key, grad_value], axis=-1))

        def pass_over(grad_query):
            return (
                grad_query,
                jnp.zeros((bucket_count, group_count, key_block, 2 * HD), jnp.float32),
            )

        return lax.cond(offset <= last_position, backward_attend, pass_over, grad_query)

    grad_query, pair_blocks = lax.scan(
        backward_block, jnp.zeros_like(attended), jnp.arange(block_count)
    )
    pair_terms = pair_blocks.transpose(1, 0, 3, 2, 4).reshape(
        bucket_count, bucket_len, group_count * 2 * HD
    )
    pair_sum = lax.psum_scatter(
        pair_terms.astype(jnp.bfloat16), "wide", scatter_dimension=1, tiled=True
    ).astype(jnp.float32)
    pair_sum = pair_sum.reshape(bucket_count, row_count, group_count, 2 * HD)
    grad_key_pre = (
        rotate_back(pair_sum[..., :HD], cosine, sine_table)
        .astype(jnp.bfloat16)
        .reshape(token_count, pair_width)
    )
    grad_value_pre = pair_sum[..., HD:].astype(jnp.bfloat16).reshape(token_count, pair_width)
    grad_query_pre = rotate_back(from_groups(grad_query, row_count), cosine, sine_table).astype(
        jnp.bfloat16
    )
    grad_query_pre = grad_query_pre.reshape(token_count, head_count * HD)
    query_grad = jnp.einsum(
        "nd,ne->de", normed_one, grad_query_pre, preferred_element_type=jnp.float32
    )
    grad_keyval = jnp.stack([grad_key_pre, grad_value_pre])
    keyval_grad = jnp.einsum(
        "nd,cne->cde", normed_one, grad_keyval, preferred_element_type=jnp.float32
    )
    normed_one_part = jnp.einsum(
        "ne,de->nd", grad_query_pre, query_weight, preferred_element_type=jnp.float32
    )
    normed_one_part = normed_one_part + jnp.einsum(
        "cne,cde->nd", grad_keyval, keyval_weight, preferred_element_type=jnp.float32
    )
    grad_normed_one = row_sum(normed_one_part)
    scaled_share = rows_of(scaled_one)
    gain_one_grad = gain_total(jnp.sum(grad_normed_one * scaled_share, axis=0))
    input_rows = grad_hidden + norm_back(
        grad_normed_one * gains[0], scaled_share, rows_of(inverse_one)
    )
    input_grad = row_collect(input_rows.astype(jnp.bfloat16)).reshape(
        bucket_count, row_count, model_width
    )
    query_sum, keyval_sum, gain_one_sum = (
        sent_and_summed(query_grad.astype(jnp.bfloat16), "wide", 0),
        sent_and_summed(keyval_grad.astype(jnp.bfloat16), "wide", 1),
        sent_and_summed(gain_one_grad.astype(jnp.bfloat16), "wide", 0),
    )
    gains_sum = jnp.stack([gain_one_sum, gain_two_sum])
    reduced = (query_sum, keyval_sum, output_sum, gateup_sum, down_sum, gains_sum)
    local_squares = jnp.sum(gains_sum * gains_sum) / narrow_count
    for matrix in reduced[:5]:
        local_squares = local_squares + jnp.sum(matrix * matrix)
    total_squares = lax.psum(local_squares, ("wide", "narrow"))
    grad_norm = jnp.sqrt(total_squares)
    factor = jnp.minimum(1.0, clip_limit / (grad_norm + 1e-06))

    def owned(weight, along):
        piece_size = weight.shape[along] // wide_count
        return lax.dynamic_slice_in_dim(weight, wide_rank * piece_size, piece_size, along).astype(
            jnp.float32
        )

    olds = (
        owned(query_weight, 0),
        owned(keyval_weight, 1),
        owned(output_weight, 1),
        owned(gateup_weight, 1),
        owned(down_weight, 1),
        owned(norm_gains, 1),
    )
    firsts = (query_first, keyval_first, output_first, gateup_first, down_first, gains_first)
    seconds = (query_second, keyval_second, output_second, gateup_second, down_second, gains_second)
    clipped = tuple((matrix * factor for matrix in reduced))
    results = []
    for number in range(6):
        step_rate = gain_rate if number == 5 else learn_rate
        decay_factor = 0.0 if number == 5 else decay_rate
        results.append(
            adam_update(
                olds[number],
                clipped[number],
                firsts[number],
                seconds[number],
                step_rate,
                decay_factor,
            )
        )
    return (
        layer_out,
        input_grad,
        clipped[0],
        clipped[1],
        clipped[2],
        clipped[3],
        clipped[4],
        clipped[5],
        grad_norm,
        results[0][1],
        results[1][1],
        results[2][1],
        results[3][1],
        results[4][1],
        results[5][1],
        results[0][2],
        results[1][2],
        results[2][2],
        results[3][2],
        results[4][2],
        results[5][2],
        results[0][0],
        results[1][0],
        results[2][0],
        results[3][0],
        results[4][0],
        results[5][0],
    )


def solution(mesh):
    return jax.shard_map(
        shards,
        mesh=mesh,
        in_specs=(
            P(None, "wide", None),
            P(None, "wide", None),
            P(),
            P(None, "narrow"),
            P(None, None, "narrow"),
            P("narrow", None),
            P(None, None, "narrow"),
            P("narrow", None),
            P(),
            P("wide", "narrow"),
            P(None, "wide", "narrow"),
            P("narrow", "wide"),
            P(None, "wide", "narrow"),
            P("narrow", "wide"),
            P(None, "wide"),
            P("wide", "narrow"),
            P(None, "wide", "narrow"),
            P("narrow", "wide"),
            P(None, "wide", "narrow"),
            P("narrow", "wide"),
            P(None, "wide"),
        ),
        out_specs=(
            P(None, "wide", None),
            P(None, "wide", None),
            P("wide", "narrow"),
            P(None, "wide", "narrow"),
            P("narrow", "wide"),
            P(None, "wide", "narrow"),
            P("narrow", "wide"),
            P(None, "wide"),
            P(),
            P("wide", "narrow"),
            P(None, "wide", "narrow"),
            P("narrow", "wide"),
            P(None, "wide", "narrow"),
            P("narrow", "wide"),
            P(None, "wide"),
            P("wide", "narrow"),
            P(None, "wide", "narrow"),
            P("narrow", "wide"),
            P(None, "wide", "narrow"),
            P("narrow", "wide"),
            P(None, "wide"),
            P("wide", "narrow"),
            P(None, "wide", "narrow"),
            P("narrow", "wide"),
            P(None, "wide", "narrow"),
            P("narrow", "wide"),
            P(None, "wide"),
        ),
        check_vma=False,
    )
```

profile of v0, /device:TPU:1, one launch (start us, length us, event | category | flops | bytes accessed | tf_op | source)
XLA Modules:
  0.0 1007.3 jit_solution(7625385558092524499)
XLA Ops:
  20.4 33.3 %all-gather.2.cloned.1.call-done = bf16[2,4096,128]{2,1,0:T(8,128)(2,1)} async-done(((bf16[2,256,128]{2,1,0:T(8,128)(2,1)}), bf16[2,4096,128]{2,1,0:T(8,128)(2,1)}) %all-gather.2.cloned.1.call-update) | async-done | bytes 2097168 | tf_op jit(solution)/shard_map/all_gather | solution.py:210
  64.1 17.1 %while.31 = (s32[]{:T(128)}, f32[2,1,1024]{2,0,1:T(2,128)S(1)}, f32[2,1,1024]{2,0,1:T(2,128)S(1)}, f32[2,1,1024,64]{2,3,0,1:T(8,128)S(1)}, s32[8]{0:T(128)S(1)},...) while((s32[]{:T(128)}, f32[2,1,1024]{2,0,1:T(2,128)S(1)}, ...), condition=%wide.region_6.7_spmd.clone, body=%wide.region_1.6_spmd.clone.sunk | while | flops 283909632 | bytes 16412001 | solution.py:265
  88.4 117.4 %reduce-scatter.15.cloned.1.call-done = bf16[64,2048]{1,0:T(8,128)(2,1)} async-done(((bf16[512,2048]{1,0:T(8,128)(2,1)}), bf16[64,2048]{1,0:T(8,128)(2,1)}) %reduce-scatter.15.cloned.1.call-update) | async-done | bytes 262160 | tf_op jit(solution)/shard_map/reduce_scatter | solution.py:138
  218.5 21.7 %all-to-all-done = bf16[8,64,2048]{2,1,0:T(8,128)(2,1)} async-done(((bf16[8,64,2048]{2,1,0:T(8,128)(2,1)}), bf16[8,64,2048]{2,1,0:T(8,128)(2,1)}, u32[]{:S(2)}, u32[]{:S(2)}) %all-to-all-start) | async-done | bytes 2097184 | tf_op jit(solution)/shard_map/all_to_all | solution.py:30
  240.2 7.7 convolution_bitcast_fusion
  251.8 9.1 bitcast_convert_fusion
  261.0 73.6 %reduce-scatter.19.cloned.1.call-done = bf16[64,2048]{1,0:T(8,128)(2,1)} async-done(((bf16[512,2048]{1,0:T(8,128)(2,1)}), bf16[64,2048]{1,0:T(8,128)(2,1)}) %reduce-scatter.19.cloned.1.call-update) | async-done | bytes 262160 | tf_op jit(solution)/shard_map/reduce_scatter | solution.py:138
  343.9 25.2 %all-to-all-done.2 = bf16[8,64,2048]{2,1,0:T(8,128)(2,1)S(1)} async-done(((bf16[8,64,2048]{2,1,0:T(8,128)(2,1)}), bf16[8,64,2048]{2,1,0:T(8,128)(2,1)S(1)}, u32[]{:S(2)}, u32[]{:S(2)}) %all-to-all-start.2) | async-done | bytes 2097184 | tf_op jit(solution)/shard_map/all_to_all | solution.py:30
  377.7 26.6 %while.32 = (s32[]{:T(128)}, f32[2,1,1024,64]{2,3,0,1:T(8,128)S(1)}, bf16[8,2,1,512,128]{4,3,0,1,2:T(8,128)(2,1)}, s32[8]{0:T(128)S(1)}, s32[]{:T(128)}, /*index...) while((s32[]{:T(128)}, ...), condition=%wide.region_16.17_spmd.clone, body=%wide.region_13.16_spmd.clone.sunk | while | flops 685114880 | bytes 24824152 | solution.py:372
  378.9 9.1 conditional.7
  408.4 118.3 %reduce-scatter.21.cloned.1.call-done = bf16[2,256,128]{2,1,0:T(8,128)(2,1)} async-done(((bf16[2,4096,128]{2,1,0:T(8,128)(2,1)}), bf16[2,256,128]{2,1,0:T(8,128)(2,1)}) %reduce-scatter.21.cloned.1.call-update) | async-done | bytes 131088 | tf_op jit(solution)/shard_map/reduce_scatter | solution.py:378
  561.3 8.4 convert_bitcast_fusion
  569.8 21.5 %copy.177 = bf16[2,2048,1024]{2,0,1:T(2,128)(2,1)} copy(bf16[2,2048,1024]{1,2,0:T(8,128)(2,1)} %convert_bitcast_fusion) | data formatting | bytes 16777216
  591.3 10.2 %copy.210 = bf16[256,8,2,1024]{3,1,2,0:T(8,128)(2,1)} copy(bf16[256,8,2,1024]{3,2,1,0:T(2,128)(2,1)} %bitcast.304) | data formatting | bytes 16777216
  604.8 8.3 all-to-all-start.4
  616.8 14.4 %all-to-all-done.4 = bf16[16,128,256]{2,1,0:T(8,128)(2,1)S(1)} async-done(((bf16[16,128,256]{2,1,0:T(8,128)(2,1)}), bf16[16,128,256]{2,1,0:T(8,128)(2,1)S(1)}, u32[]{:S(2)}, u32[]{:S(2)}) %all-to-all-start.4) | async-done | bytes 1048608 | tf_op jit(solution)/shard_map/all_to_all | solution.py:51
  637.5 35.3 %all-reduce.1 = (bf16[2048]{0:T(1024)(128)(2,1)S(1)}, bf16[2048]{0:T(1024)(128)(2,1)S(1)}) all-reduce(f32[2048]{0:T(1024)S(1)} %copy-done.39, f32[2048]{0:T(1024)S(1)} %get-tuple-element.638), channel_id=1, replica_groups=mesh['wide'=16,'narrow'=8] {'narrow'}, use_global_device_ids=true, to_apply=%region_25.26 | all-reduce | flops 4096 | bytes 24576 | tf_op jit(solution)/shard_map/psum | solution.py:148
  673.4 12.7 %all-to-all-start.5 = ((bf16[16,1,128]{2,1,0:T(2,128)(2,1)}), bf16[16,1,128]{2,1,0:T(2,128)(2,1)S(1)}, u32[]{:S(2)}, u32[]{:S(2)}) async-start(bf16[16,1,128]{2,1,0:T(2,128)(2,1)} %copy.155), calls=%async_computation.10 | async-start | bytes 16384 | tf_op jit(solution)/shard_map/all_to_all | solution.py:51
  692.7 30.5 %all_to_all.39 = bf16[8,64,2048]{2,1,0:T(8,128)(2,1)S(1)} all-to-all(bf16[8,64,2048]{2,1,0:T(8,128)(2,1)S(1)} %broadcast_in_dim.44), channel_id=1, replica_groups=mesh['wide'=16,'narrow'=8] {'narrow'}, dimensions={0} | all-to-all | bytes 4194304 | tf_op jit(solution)/shard_map/all_to_all | solution.py:30
  740.3 15.6 %reduce-scatter.25.cloned.1.call-done = bf16[128,256]{1,0:T(8,128)(2,1)} async-done(((bf16[2048,256]{1,0:T(8,128)(2,1)}), bf16[128,256]{1,0:T(8,128)(2,1)}) %reduce-scatter.25.cloned.1.call-update) | async-done | bytes 65552
  757.5 66.0 %reduce-scatter.29.cloned.1.call-done = bf16[128,1024]{1,0:T(8,128)(2,1)} async-done(((bf16[2048,1024]{1,0:T(8,128)(2,1)}), bf16[128,1024]{1,0:T(8,128)(2,1)}) %reduce-scatter.29.cloned.1.call-update) | async-done | bytes 262160
  827.1 31.1 %all-reduce = bf16[2048]{0:T(1024)(128)(2,1)S(1)} all-reduce(bf16[2048]{0:T(1024)(128)(2,1)S(1)} %get-tuple-element.690), channel_id=7, replica_groups=mesh['wide'=16,'narrow'=8] {'wide'}, use_global_device_ids=true, to_apply=%region_26.27.clone | all-reduce | flops 2048 | bytes 8192
  861.6 38.0 %reduce-scatter.27.cloned.1.call-done = bf16[128,2048]{1,0:T(8,128)(2,1)} async-done(((bf16[2048,2048]{1,0:T(8,128)(2,1)}), bf16[128,2048]{1,0:T(8,128)(2,1)}) %reduce-scatter.27.cloned.1.call-update) | async-done | bytes 524304
  903.8 68.2 %psum.23 = f32[]{:T(128)} all-reduce(f32[]{:T(128)S(6)} %add.313), channel_id=1, replica_groups=mesh['wide'=16,'narrow'=8] {'wide','narrow'}, use_global_device_ids=true, to_apply=%region_37.38 | all-reduce | flops 1 | bytes 8 | tf_op jit(solution)/shard_map/psum | solution.py:424
  (333 shorter events, 215.1 us)
Async XLA Ops:
  7.2 46.5 %all-gather.2.cloned.1.call-start = ((), (), s32[]{:S(2)}) async-start(), calls=%async_computation.15 | async-start | bytes 2228224 | tf_op jit(solution)/shard_map/all_gather | solution.py:210
  15.9 189.9 %reduce-scatter.15.cloned.1.call-start = ((), (), s32[]{:S(2)}) async-start(), calls=%async_computation.16 | async-start | bytes 2359296 | tf_op jit(solution)/shard_map/reduce_scatter | solution.py:138
  209.5 30.6 %all-to-all-start = ((bf16[8,64,2048]{2,1,0:T(8,128)(2,1)}), bf16[8,64,2048]{2,1,0:T(8,128)(2,1)}, u32[]{:S(2)}, u32[]{:S(2)}) async-start(bf16[8,64,2048]{2,1,0:T(8,128)(2,1)} %broadcast_in_dim.40), calls=%async_computation.1 | async-start | bytes 4194304 | tf_op jit(solution)/shard_map/all_to_all | solution.py:30
  214.0 120.6 %reduce-scatter.19.cloned.1.call-start = ((), (), s32[]{:S(2)}) async-start(), calls=%async_computation.18 | async-start | bytes 2359296 | tf_op jit(solution)/shard_map/reduce_scatter | solution.py:138
  260.9 73.7 %copy-start.32 = (f32[1,2048]{1,0:T(1,128)S(1)}, f32[1,2048]{1,0:T(1,128)}, u32[]{:S(2)}) copy-start(f32[1,2048]{1,0:T(1,128)} %get-tuple-element.738) | copy-start | bytes 24580
  260.9 73.7 %copy-start.44 = (f32[64]{0:T(128)S(1)}, f32[64]{0:T(128)}, u32[]{:S(2)}) copy-start(f32[64]{0:T(128)} %copy-done.43) | copy-start | bytes 772
  339.3 29.8 %all-to-all-start.2 = ((bf16[8,64,2048]{2,1,0:T(8,128)(2,1)}), bf16[8,64,2048]{2,1,0:T(8,128)(2,1)S(1)}, u32[]{:S(2)}, u32[]{:S(2)}) async-start(bf16[8,64,2048]{2,1,0:T(8,128)(2,1)} %broadcast_in_dim.43), calls=%async_computation.5 | async-start | bytes 4194304 | tf_op jit(solution)/shard_map/all_to_all | solution.py:30
  343.1 183.6 %reduce-scatter.21.cloned.1.call-start = ((), (), s32[]{:S(2)}) async-start(), calls=%async_computation.19 | async-start | bytes 2228224 | tf_op jit(solution)/shard_map/reduce_scatter | solution.py:378
  404.4 231.8 %reduce-scatter.23.cloned.1.call-start = ((), (), s32[]{:S(2)}) async-start(), calls=%async_computation.20 | async-start | bytes 2359296 | tf_op jit(solution)/shard_map/reduce_scatter | solution.py:138
  405.6 123.2 %copy-start.18 = (f32[256,32]{1,0:T(8,128)S(1)}, f32[256,32]{1,0:T(8,128)}, u32[]{:S(2)}) copy-start(f32[256,32]{1,0:T(8,128)} %copy-done.17) | copy-start | bytes 98308
  408.4 120.7 %copy-start.11 = (bf16[2,2048,64]{1,2,0:T(8,128)(2,1)S(1)}, bf16[2,2048,64]{1,2,0:T(8,128)(2,1)}, u32[]{:S(2)}) copy-start(bf16[2,2048,64]{1,2,0:T(8,128)(2,1)} %param.33) | copy-start | bytes 1572868
  533.4 157.4 %reduce-scatter.17.cloned.1.call-start = ((), (), s32[]{:S(2)}) async-start(), calls=%async_computation.17 | async-start | bytes 2359296 | tf_op jit(solution)/shard_map/reduce_scatter | solution.py:138
  540.7 215.3 %reduce-scatter.25.cloned.1.call-start = ((), (), s32[]{:S(2)}) async-start(), calls=%async_computation.21 | async-start | bytes 1114112
  546.3 277.2 %reduce-scatter.29.cloned.1.call-start = ((), (), s32[]{:S(2)}) async-start(), calls=%async_computation.23 | async-start | bytes 4456448
  559.8 339.8 %reduce-scatter.27.cloned.1.call-start = ((), (), s32[]{:S(2)}) async-start(), calls=%async_computation.22 | async-start | bytes 8912896
  604.8 26.3 %all-to-all-start.4 = ((bf16[16,128,256]{2,1,0:T(8,128)(2,1)}), bf16[16,128,256]{2,1,0:T(8,128)(2,1)S(1)}, u32[]{:S(2)}, u32[]{:S(2)}) async-start(bf16[16,128,256]{2,1,0:T(8,128)(2,1)} %bitcast.328), calls=%async_computation.9 | async-start | bytes 2097152 | tf_op jit(solution)/shard_map/all_to_all | solution.py:51
  615.8 75.0 %copy-start.9 = (bf16[64,2048]{1,0:T(8,128)(2,1)S(1)}, bf16[64,2048]{1,0:T(8,128)(2,1)}, u32[]{:S(2)}) copy-start(bf16[64,2048]{1,0:T(8,128)(2,1)} %reduce-scatter.19.cloned.1.call-done) | copy-start | bytes 786436
  615.8 75.0 %copy-start.33 = (f32[1,2048]{1,0:T(1,128)S(1)}, f32[1,2048]{1,0:T(1,128)}, u32[]{:S(2)}) copy-start(f32[1,2048]{1,0:T(1,128)} %get-tuple-element.738) | copy-start | bytes 24580
  615.8 75.0 %copy-start.45 = (f32[64]{0:T(128)S(1)}, f32[64]{0:T(128)}, u32[]{:S(2)}) copy-start(f32[64]{0:T(128)} %copy-done.43) | copy-start | bytes 772
  615.8 75.0 %copy-start.47 = (f32[64]{0:T(128)S(1)}, f32[64]{0:T(128)}, u32[]{:S(2)}) copy-start(f32[64]{0:T(128)} %copy-done.46) | copy-start | bytes 772
  631.1 42.3 %all-to-all-start.6 = ((bf16[16,2,128,64]{2,3,1,0:T(8,128)(2,1)}), bf16[16,2,128,64]{2,3,1,0:T(8,128)(2,1)S(1)}, u32[]{:S(2)}, u32[]{:S(2)}) async-start(bf16[16,2,128,64]{2,3,1,0:T(8,128)(2,1)} %bitcast.296), calls=%async_computation.11 | async-start | bytes 1048576 | tf_op jit(solution)/shard_map/all_to_all | solution.py:51
  673.4 19.1 %all-to-all-start.5 = ((bf16[16,1,128]{2,1,0:T(2,128)(2,1)}), bf16[16,1,128]{2,1,0:T(2,128)(2,1)S(1)}, u32[]{:S(2)}, u32[]{:S(2)}) async-start(bf16[16,1,128]{2,1,0:T(2,128)(2,1)} %copy.155), calls=%async_computation.10 | async-start | bytes 16384 | tf_op jit(solution)/shard_map/all_to_all | solution.py:51
  724.8 179.0 %all-to-all-start.1 = ((bf16[8,64,2048]{2,1,0:T(8,128)(2,1)}), bf16[8,64,2048]{2,1,0:T(8,128)(2,1)}, u32[]{:S(2)}, u32[]{:S(2)}) async-start(bf16[8,64,2048]{2,1,0:T(8,128)(2,1)} %broadcast_in_dim.41), calls=%async_computation.3 | async-start | bytes 4194304 | tf_op jit(solution)/shard_map/all_to_all | solution.py:30
  826.5 74.5 %copy-start.20 = (f32[2,128,64]{1,2,0:T(8,128)}, f32[2,128,64]{1,2,0:T(8,128)S(1)}, u32[]{:S(2)}) copy-start(f32[2,128,64]{1,2,0:T(8,128)S(1)} %convert_reduce_fusion.1) | copy-start | bytes 196612
  (47 other events, 275.0 us)
Sparse Core Ops, SparseCore 0:
  16.0 37.5 all-gather.1
  85.8 119.9 reduce-scatter.14
  261.1 73.4 reduce-scatter.18
  404.5 122.1 reduce-scatter.20
  533.5 76.0 reduce-scatter.22
  613.2 77.5 reduce-scatter.16
  693.7 62.1 reduce-scatter.24
  758.5 65.0 reduce-scatter.28
  826.1 73.5 reduce-scatter.26
where the time goes:
time: 1020 us; the launch traced here: 1010 us
  waiting for transfers between devices  528 us (52%)
  blocking collectives  165 us (16%)
  local copies, waits for them, and re-layouts  121 us (12%)
  matrix products  76.9 us (8%)
  other arithmetic  43 us (4%)
  starting transfers between devices  39.9 us (4%)
  between operations  21.5 us (2%)
  loops' own time  11.3 us (1%)
    reduce_scatter x4, waiting for transfers between devices, row_sum(): lax.psum_scatter(values.astype(jnp.bfloat16), 'narrow', scatter_dimension...  196 us
    unnamed x12, waiting for transfers between devices  120 us
    reduce_scatter x1, waiting for transfers between devices, shards(): lax.psum_scatter(pair_terms.astype(jnp.bfloat16), 'wide', scatter_dimensi...  118 us
    unnamed x137, local copies, waits for them, and re-layouts  82.9 us
    psum x1, blocking collectives, shards(): total_squares = lax.psum(local_squares, ('wide', 'narrow'))  68.2 us
    all_to_all x3, waiting for transfers between devices, sent_to_all(): lax.all_to_all(jnp.broadcast_to(x[None], (peers, *x.shape)), axis, 0, 0,...  46.9 us
    psum x1, blocking collectives, gain_total(): return lax.psum(values, 'narrow')  35.3 us
    all_gather x1, waiting for transfers between devices, shards(): all_pairs = lax.all_gather(local_pairs, 'wide', axis=1, tiled=True)  33.3 us
  transfers between devices with their start and end apart: 15, of which 11 were waited for; matrix products, arithmetic and copies ran while one was open for 11% of the time, Pallas kernels for 0%

commit v1 on v0

v1 whole, which is shorter than its diff:
```python
import functools
import math

import jax
import jax.numpy as jnp
from jax import lax
from jax.experimental import pallas as pl
from jax.experimental.pallas import tpu as pltpu
from jax.sharding import PartitionSpec as P

HD = 64
STEP = 10


norm_eps = 1e-05
rope_theta = 500000.0
rope_factor = 32.0
rope_low = 1.0
rope_high = 4.0
rope_context = 8192.0
clip_limit = 1.0
beta_first = 0.9
beta_second = 0.95
adam_eps = 1e-08
learn_rate = 0.09
gain_rate = 1.2
decay_rate = 0.1
masked_score = -1e30


bf16 = jnp.bfloat16
f32 = jnp.float32
MESH = pl.DeviceIdType.MESH
MB = 1024 * 1024


def dot_nn(a, b):
    return jnp.dot(a, b, preferred_element_type=f32)


def dot_nt(a, b):
    return lax.dot_general(a, b, (((1,), (1,)), ((), ())), preferred_element_type=f32)


def dot_tn(a, b):
    return lax.dot_general(a, b, (((0,), (0,)), ((), ())), preferred_element_type=f32)


def greet(targets):
    barrier = pltpu.get_barrier_semaphore()
    for target in targets:
        pl.semaphore_signal(barrier, inc=1, device_id=target, device_id_type=MESH)
    pl.semaphore_wait(barrier, len(targets))


def tile(j, size):
    return pl.ds(pl.multiple_of(j * size, size), size)


def middle_kernel(
    peers,
    chunks,
    ob_ref,
    wo_hbm,
    tok_ref,
    dy_ref,
    dyb_hbm,
    gains_ref,
    wgu_hbm,
    wd_hbm,
    hidden_ref,
    ffsum_ref,
    dob_ref,
    dh_ref,
    gain_ref,
    gout_hbm,
    ggu_hbm,
    gdown_hbm,
    wo,
    wgu,
    wd,
    dyb,
    da,
    n2,
    dgu,
    mixed,
    dhb,
    send,
    recv,
    send2,
    recv2,
    send3,
    recv3,
    gout,
    ggu,
    gdown,
    in_sem,
    out_sem,
    s_sem,
    r_sem,
    s_sem2,
    r_sem2,
    s_sem3,
    r_sem3,
):
    me = lax.axis_index("narrow")
    wide_me = lax.axis_index("wide")
    rows = tok_ref.shape[0]
    width = tok_ref.shape[1]
    units = wd.shape[0]
    span = 256
    peer = [(wide_me, lax.rem(me + step, peers)) for step in range(1, peers)]
    loads = [
        pltpu.make_async_copy(wo_hbm, wo, in_sem.at[0]),
        pltpu.make_async_copy(wd_hbm, wd, in_sem.at[1]),
        pltpu.make_async_copy(dyb_hbm, dyb, in_sem.at[2]),
        pltpu.make_async_copy(wgu_hbm, wgu, in_sem.at[3]),
    ]
    for load in loads:
        load.start()
    greet(peer)

    def send_block(slot, src, dst, ssem, rsem):
        copy = pltpu.make_async_remote_copy(
            src_ref=src, dst_ref=dst, send_sem=ssem, recv_sem=rsem,
            device_id=peer[slot], device_id_type=MESH,
        )
        copy.start()
        return copy

    loads[0].wait()
    flight = []
    for slot in range(peers - 1):
        theirs = pl.ds(pl.multiple_of(peer[slot][1] * rows, rows), rows)
        send[slot] = dot_nn(ob_ref[theirs, :], wo[...]).astype(bf16)
        flight.append(send_block(slot, send.at[slot], recv.at[slot], s_sem.at[0, slot], r_sem.at[0, slot]))
    mine = pl.ds(pl.multiple_of(me * rows, rows), rows)
    hidden = tok_ref[...].astype(f32) + dot_nn(ob_ref[mine, :], wo[...])
    loads[1].wait()
    loads[2].wait()

    def grad_middle(j, carry):
        da[:, tile(j, span)] = dot_nt(dyb[...], wd[tile(j, span), :])
        return carry

    lax.fori_loop(0, units // span, grad_middle, 0)
    for copy in flight:
        copy.wait_recv()
    for slot in range(peers - 1):
        hidden = hidden + recv[slot].astype(f32)
    hidden_ref[...] = hidden
    inverse = lax.rsqrt(jnp.mean(hidden * hidden, axis=-1, keepdims=True) + norm_eps)
    gain2 = gains_ref[1:2, :].astype(f32)
    n2[mine, :] = (hidden * inverse * gain2).astype(bf16)
    for copy in flight:
        copy.wait_send()
    flight = [
        send_block(slot, n2.at[mine, :], n2.at[mine, :], s_sem.at[1, slot], r_sem.at[1, slot])
        for slot in range(peers - 1)
    ]
    loads[3].wait()
    for copy in flight:
        copy.wait()

    def gate_up(j, carry):
        gate = dot_nn(n2[...], wgu[0, :, tile(j, span)])
        up = dot_nn(n2[...], wgu[1, :, tile(j, span)])
        sigmoid = jax.nn.sigmoid(gate)
        activated = gate * sigmoid
        mixed[:, tile(j, span)] = (activated * up).astype(bf16)
        grad = da[:, tile(j, span)]
        dgu[0, :, tile(j, span)] = (
            grad * up * sigmoid * (1.0 + gate * (1.0 - sigmoid))
        ).astype(bf16)
        dgu[1, :, tile(j, span)] = (grad * activated).astype(bf16)
        return carry

    lax.fori_loop(0, units // span, gate_up, 0)

    chunk = width // chunks

    def scatter(out, into, ssem, rsem, product):
        def per_chunk(c, carry):
            columns = tile(c, chunk)
            out[:, columns] = product(c).astype(bf16)
            for slot in range(peers - 1):
                theirs = pl.ds(pl.multiple_of(peer[slot][1] * rows, rows), rows)
                send_block(
                    slot, out.at[theirs, columns], into.at[slot, :, columns],
                    ssem.at[slot, c], rsem.at[slot, c],
                )
            return carry

        lax.fori_loop(0, chunks, per_chunk, 0)

    def scatter_wait(out, into, ssem, rsem):
        def per_chunk(c, carry):
            columns = tile(c, chunk)
            for slot in range(peers - 1):
                theirs = pl.ds(pl.multiple_of(peer[slot][1] * rows, rows), rows)
                pltpu.make_async_remote_copy(
                    src_ref=out.at[theirs, columns], dst_ref=into.at[slot, :, columns],
                    send_sem=ssem.at[slot, c], recv_sem=rsem.at[slot, c],
                    device_id=peer[slot], device_id_type=MESH,
                ).wait()
            return carry

        lax.fori_loop(0, chunks, per_chunk, 0)

    scatter(
        send2, recv2, s_sem2, r_sem2,
        lambda c: dot_nt(dgu[0], wgu[0, tile(c, chunk), :]) + dot_nt(dgu[1], wgu[1, tile(c, chunk), :]),
    )
    scatter(send3, recv3, s_sem3, r_sem3, lambda c: dot_nn(mixed[...], wd[:, tile(c, chunk)]))

    def grad_gateup(j, carry):
        which = lax.div(j, width // span)
        part = lax.rem(j, width // span)
        ggu[which, tile(part, span), :] = dot_tn(n2[:, tile(part, span)], dgu[which]).astype(bf16)
        return carry

    lax.fori_loop(0, 2 * (width // span), grad_gateup, 0)
    store_gu = pltpu.make_async_copy(ggu, ggu_hbm, out_sem.at[0])
    store_gu.start()

    scatter_wait(send2, recv2, s_sem2, r_sem2)
    total = send2[mine, :].astype(f32)
    for slot in range(peers - 1):
        total = total + recv2[slot].astype(f32)
    z2 = hidden_ref[...] * inverse
    gain_ref[...] = jnp.broadcast_to(jnp.sum(total * z2, axis=0, keepdims=True), gain_ref.shape)
    weighted = total * gain2
    dh = dy_ref[...].astype(f32) + inverse * (
        weighted - z2 * jnp.mean(weighted * z2, axis=-1, keepdims=True)
    )
    dh_ref[...] = dh
    dhb[mine, :] = dh.astype(bf16)
    flight = [
        send_block(slot, dhb.at[mine, :], dhb.at[mine, :], s_sem.at[2, slot], r_sem.at[2, slot])
        for slot in range(peers - 1)
    ]

    def grad_down(j, carry):
        gdown[tile(j, span), :] = dot_tn(mixed[:, tile(j, span)], dyb[...]).astype(bf16)
        return carry

    lax.fori_loop(0, units // span, grad_down, 0)
    store_down = pltpu.make_async_copy(gdown, gdown_hbm, out_sem.at[1])
    store_down.start()
    for copy in flight:
        copy.wait()
    dob_ref[...] = dot_nt(dhb[...], wo[...]).astype(bf16)

    def grad_out(j, carry):
        gout[:, tile(j, span)] = dot_tn(ob_ref[...], dhb[:, tile(j, span)]).astype(bf16)
        return carry

    lax.fori_loop(0, width // span, grad_out, 0)
    store_out = pltpu.make_async_copy(gout, gout_hbm, out_sem.at[2])
    store_out.start()
    scatter_wait(send3, recv3, s_sem3, r_sem3)
    total = send3[mine, :].astype(f32)
    for slot in range(peers - 1):
        total = total + recv3[slot].astype(f32)
    ffsum_ref[...] = (hidden_ref[...] + total).astype(bf16)
    store_gu.wait()
    store_down.wait()
    store_out.wait()


def middle(peers, ob, wo, tok_rows, dy_rows, dyb, gains, wgu, wd):
    tokens, width = dyb.shape
    rows = tok_rows.shape[0]
    units = wd.shape[0]
    heads = wo.shape[0]
    chunks = 4
    anywhere = pl.BlockSpec(memory_space=pl.ANY)
    here = pl.BlockSpec(memory_space=pltpu.VMEM)
    shape = jax.ShapeDtypeStruct
    dma = pltpu.SemaphoreType.DMA
    return pl.pallas_call(
        functools.partial(middle_kernel, peers, chunks),
        out_shape=(
            shape((rows, width), f32),
            shape((rows, width), bf16),
            shape((tokens, heads), bf16),
            shape((rows, width), f32),
            shape((8, width), f32),
            shape((heads, width), bf16),
            shape((2, width, units), bf16),
            shape((units, width), bf16),
        ),
        in_specs=[here, anywhere, here, here, anywhere, here, anywhere, anywhere],
        out_specs=(here, here, here, here, here, anywhere, anywhere, anywhere),
        scratch_shapes=[
            pltpu.VMEM(wo.shape, bf16),
            pltpu.VMEM(wgu.shape, bf16),
            pltpu.VMEM(wd.shape, bf16),
            pltpu.VMEM((tokens, width), bf16),
            pltpu.VMEM((tokens, units), f32),
            pltpu.VMEM((tokens, width), bf16),
            pltpu.VMEM((2, tokens, units), bf16),
            pltpu.VMEM((tokens, units), bf16),
            pltpu.VMEM((tokens, width), bf16),
            pltpu.VMEM((peers - 1, rows, width), bf16),
            pltpu.VMEM((peers - 1, rows, width), bf16),
            pltpu.VMEM((tokens, width), bf16),
            pltpu.VMEM((peers - 1, rows, width), bf16),
            pltpu.VMEM((tokens, width), bf16),
            pltpu.VMEM((peers - 1, rows, width), bf16),
            pltpu.VMEM((heads, width), bf16),
            pltpu.VMEM((2, width, units), bf16),
            pltpu.VMEM((units, width), bf16),
            dma((4,)),
            dma((3,)),
            dma((3, peers - 1)),
            dma((3, peers - 1)),
            dma((peers - 1, chunks)),
            dma((peers - 1, chunks)),
            dma((peers - 1, chunks)),
            dma((peers - 1, chunks)),
        ],
        compiler_params=pltpu.CompilerParams(
            collective_id=1, has_side_effects=True, vmem_limit_bytes=63 * MB
        ),
        name="middle",
    )(ob, wo, tok_rows, dy_rows, dyb, gains, wgu, wd)


def swap_halves(u):
    half = HD // 2
    width = u.shape[-1]
    lane = lax.broadcasted_iota(jnp.int32, u.shape, u.ndim - 1)
    ahead = pltpu.roll(u, width - half, u.ndim - 1)
    behind = pltpu.roll(u, half, u.ndim - 1)
    return jnp.where(lax.rem(lane, HD) < half, ahead, behind)


def front_kernel(
    others, tok_ref, gains_ref, wq_ref, wkv_ref, cos_ref, sin_ref,
    n1_ref, q_ref, kv_ref, s_sem, r_sem, f_s_sem, f_r_sem,
):
    narrow_me = lax.axis_index("narrow")
    me = lax.axis_index("wide")
    chips = others + 1
    chip, core = lax.div(me, 2), lax.rem(me, 2)
    chip_of = [lax.rem(chip + step, chips) for step in range(1, chips)]
    peer = [(2 * there + core, narrow_me) for there in chip_of]
    mate = (2 * chip + 1 - core, narrow_me)
    greet(peer + [mate])
    tokens, width = tok_ref.shape
    span = 64

    def normed(j, carry):
        rows = tile(j, span)
        values = tok_ref[rows, :].astype(f32)
        inverse = lax.rsqrt(jnp.mean(values * values, axis=-1, keepdims=True) + norm_eps)
        n1_ref[rows, :] = (values * inverse * gains_ref[0:1, :].astype(f32)).astype(bf16)
        return carry

    lax.fori_loop(0, tokens // span, normed, 0)
    lane = lax.broadcasted_iota(jnp.int32, (tokens, 2 * HD), 1)
    cosine, sine = cos_ref[...], sin_ref[...]
    kv = dot_nn(n1_ref[...], wkv_ref[...])
    turned = kv * cosine + swap_halves(kv) * sine
    kv_ref[me] = jnp.where(lane < HD, turned, kv).astype(bf16)

    def send(src, there, ssem, rsem):
        copy = pltpu.make_async_remote_copy(
            src_ref=src, dst_ref=src, send_sem=ssem, recv_sem=rsem,
            device_id=there, device_id_type=MESH,
        )
        copy.start()
        return copy

    flight = [
        send(kv_ref.at[me], peer[step], s_sem.at[step], r_sem.at[step]) for step in range(others)
    ]
    to_mate = [send(kv_ref.at[me], mate, f_s_sem.at[others], f_r_sem.at[others])]
    for pair in range(wq_ref.shape[1] // (2 * HD)):
        columns = pl.ds(pair * 2 * HD, 2 * HD)
        query = dot_nn(n1_ref[...], wq_ref[:, columns])
        q_ref[:, columns] = ((query * cosine + swap_halves(query) * sine) * HD**-0.5).astype(bf16)
    for step in range(others):
        arrived = lax.rem(chip + chips - 1 - step, chips)
        flight[step].wait_recv()
        block = kv_ref.at[2 * arrived + core]
        to_mate.append(send(block, mate, f_s_sem.at[step], f_r_sem.at[step]))
    for copy in flight:
        copy.wait_send()
    for copy in to_mate:
        copy.wait()


def front(wide_count, tokens, gains, wq, wkv, cosine, sine):
    count, width = tokens.shape
    others = wide_count // 2 - 1
    here = pl.BlockSpec(memory_space=pltpu.VMEM)
    shape = jax.ShapeDtypeStruct
    dma = pltpu.SemaphoreType.DMA
    return pl.pallas_call(
        functools.partial(front_kernel, others),
        out_shape=(
            shape((count, width), bf16),
            shape((count, wq.shape[1]), bf16),
            shape((wide_count, count, 2 * HD), bf16),
        ),
        in_specs=[here] * 6,
        out_specs=(here, here, here),
        scratch_shapes=[dma((others,)), dma((others,)), dma((others + 1,)), dma((others + 1,))],
        compiler_params=pltpu.CompilerParams(
            collective_id=2, has_side_effects=True, vmem_limit_bytes=48 * MB
        ),
        name="front",
    )(tokens, gains, wq, wkv, cosine, sine)


def wide_rows(block):
    return block.reshape(block.shape[0] * block.shape[1], block.shape[2])


def head_lanes(ref, rows, head, high):
    pair = ref[rows, pl.ds((head // 2) * 2 * HD, 2 * HD)].astype(f32)
    lane = lax.broadcasted_iota(jnp.int32, pair.shape, 1)
    if (head % 2 == 1) != high:
        pair = pltpu.roll(pair, HD, 1)
    return jnp.where((lane >= HD) == high, pair, 0.0)


def attend_kernel(blocks, len_ref, q_ref, kv_ref, ob_ref, o_ref, log_ref, head_q):
    me = lax.axis_index("wide")
    rows_each = kv_ref.shape[1] // 2
    heads = q_ref.shape[1] // HD
    key_span = blocks * rows_each
    first = me * rows_each
    for bucket in range(2):
        rows = pl.ds(bucket * rows_each, rows_each)
        for head in range(heads):
            head_q[head] = head_lanes(q_ref, rows, head, False).astype(bf16)
        length = len_ref[bucket]
        whole = lax.div(jnp.minimum(first, length), key_span)
        last = lax.div(jnp.minimum(first + rows_each, length) + key_span - 1, key_span)

        def step(masked, index, carry):
            block = wide_rows(kv_ref[pl.ds(index * blocks, blocks), rows, :])
            lane = lax.broadcasted_iota(jnp.int32, block.shape, 1)
            ones_v = jnp.where(lane < HD, jnp.ones_like(block), block)
            if masked:
                key = index * key_span + lax.broadcasted_iota(jnp.int32, (rows_each, key_span), 1)
                place = first + lax.broadcasted_iota(jnp.int32, (rows_each, key_span), 0)
                allowed = (key <= place) & (key < length)
            result = []
            for head in range(heads):
                best, total = carry[head]
                scores = dot_nt(head_q[head], block)
                if masked:
                    scores = jnp.where(allowed, scores, masked_score)
                new_best = jnp.maximum(best, jnp.max(scores, axis=-1, keepdims=True))
                weights = jnp.exp(scores - new_best).astype(bf16)
                total = total * jnp.exp(best - new_best) + dot_nn(weights, ones_v)
                result.append((new_best, total))
            return tuple(result)

        carry = tuple(
            (jnp.full((rows_each, 1), masked_score, f32), jnp.zeros((rows_each, 2 * HD), f32))
            for _ in range(heads)
        )
        carry = lax.fori_loop(0, whole, functools.partial(step, False), carry)
        carry = lax.fori_loop(whole, last, functools.partial(step, True), carry)
        lane = lax.broadcasted_iota(jnp.int32, (rows_each, 2 * HD), 1)
        outs = []
        for head in range(heads):
            best, total = carry[head]
            sums = jnp.where(lane < HD, total, pltpu.roll(total, HD, 1))
            log_row = jnp.transpose(best + jnp.log(sums))
            log_ref[pl.ds(bucket * heads + head, 1), :] = log_row[0:1, :]
            outs.append(total / sums)
        for pair in range(heads // 2):
            value = jnp.where(lane < HD, pltpu.roll(outs[2 * pair], HD, 1), outs[2 * pair + 1])
            columns = pl.ds(pair * 2 * HD, 2 * HD)
            o_ref[rows, columns] = value
            ob_ref[rows, columns] = value.astype(bf16)


def attend(lengths, queries, pairs):
    shape = jax.ShapeDtypeStruct
    here = pl.BlockSpec(memory_space=pltpu.VMEM)
    rows_each = queries.shape[0] // 2
    heads = queries.shape[1] // HD
    return pl.pallas_call(
        functools.partial(attend_kernel, 2),
        out_shape=(
            shape(queries.shape, bf16), shape(queries.shape, f32), shape((2 * heads, rows_each), f32),
        ),
        in_specs=[pl.BlockSpec(memory_space=pltpu.SMEM), here, here],
        out_specs=(here, here, here),
        scratch_shapes=[pltpu.VMEM((heads, rows_each, 2 * HD), bf16)],
        compiler_params=pltpu.CompilerParams(vmem_limit_bytes=48 * MB),
        name="attend",
    )(lengths, queries, pairs)


def attend_back_kernel(
    blocks, len_ref, q_ref, kv_ref, o_ref, log_ref, dob_ref, cos_ref, sin_ref,
    dq_ref, dkv_ref, head_q, head_do, delta, grad,
):
    me = lax.axis_index("wide")
    rows_each = kv_ref.shape[1] // 2
    heads = q_ref.shape[1] // HD
    key_span = blocks * rows_each
    first = me * rows_each

    def clear(index, carry):
        dkv_ref[index] = jnp.zeros(dkv_ref.shape[1:], bf16)
        return carry

    lax.fori_loop(0, dkv_ref.shape[0], clear, 0)
    for bucket in range(2):
        rows = pl.ds(bucket * rows_each, rows_each)
        for head in range(heads):
            head_q[head] = head_lanes(q_ref, rows, head, False).astype(bf16)
            upper = head_lanes(dob_ref, rows, head, True)
            head_do[head] = upper.astype(bf16)
            product = upper * head_lanes(o_ref, rows, head, True)
            delta[pl.ds(head, 1), :] = jnp.sum(jnp.transpose(product), axis=0, keepdims=True)
            grad[head] = jnp.zeros((rows_each, 2 * HD), f32)
        length = len_ref[bucket]
        whole = lax.div(jnp.minimum(first, length), key_span)
        last = lax.div(jnp.minimum(first + rows_each, length) + key_span - 1, key_span)
        last = jnp.where(first < length, last, 0)
        whole = jnp.minimum(whole, last)

        def step(masked, index, carry):
            block = wide_rows(kv_ref[pl.ds(index * blocks, blocks), rows, :])
            if masked:
                key = index * key_span + lax.broadcasted_iota(jnp.int32, (key_span, rows_each), 0)
                place = first + lax.broadcasted_iota(jnp.int32, (key_span, rows_each), 1)
                allowed = (key <= place) & (key < length)
            total = jnp.zeros((key_span, 2 * HD), f32)
            for head in range(heads):
                scores = dot_nt(block, head_q[head])
                if masked:
                    scores = jnp.where(allowed, scores, masked_score)
                chances = jnp.exp(scores - log_ref[pl.ds(bucket * heads + head, 1), :])
                slope = dot_nt(block, head_do[head]) - delta[pl.ds(head, 1), :]
                slope = (chances * slope).astype(bf16)
                total = total + dot_nn(slope, head_q[head]) + dot_nn(chances.astype(bf16), head_do[head])
                grad[head] = grad[head] + dot_tn(slope, block)
            dkv_ref[pl.ds(index * blocks, blocks), rows, :] = total.astype(bf16).reshape(
                blocks, rows_each, 2 * HD
            )
            return carry

        lax.fori_loop(0, whole, functools.partial(step, False), 0)
        lax.fori_loop(whole, last, functools.partial(step, True), 0)
        lane = lax.broadcasted_iota(jnp.int32, (rows_each, 2 * HD), 1)
        for pair in range(heads // 2):
            value = jnp.where(lane < HD, grad[2 * pair], pltpu.roll(grad[2 * pair + 1], HD, 1))
            value = value * HD**-0.5
            turned = value * cos_ref[rows, :] - swap_halves(value) * sin_ref[rows, :]
            dq_ref[rows, pl.ds(pair * 2 * HD, 2 * HD)] = turned.astype(bf16)


def attend_back(lengths, queries, pairs, out, logs, grad_out, cosine, sine):
    shape = jax.ShapeDtypeStruct
    here = pl.BlockSpec(memory_space=pltpu.VMEM)
    rows_each = queries.shape[0] // 2
    heads = queries.shape[1] // HD
    return pl.pallas_call(
        functools.partial(attend_back_kernel, 2),
        out_shape=(shape(queries.shape, bf16), shape(pairs.shape, bf16)),
        in_specs=[pl.BlockSpec(memory_space=pltpu.SMEM)] + [here] * 7,
        out_specs=(here, here),
        scratch_shapes=[
            pltpu.VMEM((heads, rows_each, 2 * HD), bf16),
            pltpu.VMEM((heads, rows_each, 2 * HD), bf16),
            pltpu.VMEM((heads, rows_each), f32),
            pltpu.VMEM((heads, rows_each, 2 * HD), f32),
        ],
        compiler_params=pltpu.CompilerParams(vmem_limit_bytes=48 * MB),
        name="attend_back",
    )(lengths, queries, pairs, out, logs, grad_out, cosine, sine)


class Item:
    def __init__(self, source, loaded, mate_in, own, chip_in, sems):
        self.source, self.loaded = source, loaded
        self.mate_in, self.own, self.chip_in = mate_in, own, chip_in
        self.s1, self.r1, self.s2, self.r2, self.ld = sems


def wide_place():
    me = lax.axis_index("wide")
    return lax.div(me, 2), lax.rem(me, 2)


def item_chip(k, chips):
    chip, _ = wide_place()
    return lax.rem(chip + 1 + k, chips)


def to_mate(item, k, chips):
    chip, core = wide_place()
    there = item_chip(k, chips)
    return pltpu.make_async_remote_copy(
        src_ref=item.source(2 * there + 1 - core), dst_ref=item.mate_in.at[k],
        send_sem=item.s1.at[k], recv_sem=item.r1.at[k],
        device_id=(2 * chip + 1 - core, lax.axis_index("narrow")), device_id_type=MESH,
    )


def own_load(item, k, chips):
    _, core = wide_place()
    there = item_chip(k, chips)
    return pltpu.make_async_copy(item.source(2 * there + core), item.own.at[k], item.ld.at[k])


def to_chip(item, k, chips):
    _, core = wide_place()
    there = item_chip(k, chips)
    return pltpu.make_async_remote_copy(
        src_ref=item.own.at[k], dst_ref=item.chip_in.at[k],
        send_sem=item.s2.at[k], recv_sem=item.r2.at[k],
        device_id=(2 * there + core, lax.axis_index("narrow")), device_id_type=MESH,
    )


def stage_one(item, chips):
    def per_block(k, carry):
        to_mate(item, k, chips).start()
        own_load(item, k, chips).start()
        return carry

    lax.fori_loop(0, chips, per_block, 0)


def add_mate(item, k, chips):
    to_mate(item, k, chips).wait_recv()
    own_load(item, k, chips).wait()
    item.own[k] = (item.own[k].astype(f32) + item.mate_in[k].astype(f32)).astype(bf16)


def stage_two(item, chips):
    def per_block(k, carry):
        add_mate(item, k, chips)
        to_chip(item, k, chips).start()
        return carry

    lax.fori_loop(0, chips - 1, per_block, 0)
    add_mate(item, chips - 1, chips)


def arrive(item, chips):
    def per_block(k, carry):
        to_chip(item, k, chips).wait_recv()
        return carry

    lax.fori_loop(0, chips - 1, per_block, 0)


def drain(item, chips):
    def per_block(k, carry):
        to_mate(item, k, chips).wait_send()
        return carry

    def per_chip(k, carry):
        to_chip(item, k, chips).wait_send()
        return carry

    lax.fori_loop(0, chips, per_block, 0)
    lax.fori_loop(0, chips - 1, per_chip, 0)


def block_total(item, rows, chips):
    total = item.own[chips - 1, rows, :].astype(f32)
    for k in range(chips - 1):
        total = total + item.chip_in[k, rows, :].astype(f32)
    return total


def finish(item, out_ref, chips):
    height, breadth = out_ref.shape
    span = max(8, min(height, 32768 // breadth))

    def per_tile(j, squares):
        rows = tile(j, span)
        total = block_total(item, rows, chips)
        out_ref[rows, :] = total
        return squares + jnp.sum(total * total, axis=0, keepdims=True)

    squares = lax.fori_loop(0, height // span, per_tile, jnp.zeros((1, breadth), f32))
    return jnp.sum(squares, axis=1, keepdims=True)


def last_kernel(
    peers, chips, chunks,
    dkv_ref, dq_ref, n1_ref, tok_ref, gains_ref, wq_ref, wkv_ref, dh_ref, rows_ref, gain2_ref,
    cos_ref, sin_ref, gout_hbm, ggu_hbm, gdown_hbm,
    layer_ref, grad_ref, q_ref, kv_ref, out_ref, gu_ref, down_ref, gains_out_ref, norm_ref,
    dkv, gq, gkv, send, recv, gain_part, gain_mate, gain_in, gain_near, norm_own, norm_mate, norm_in,
    *rest,
):
    buffers, rest = rest[: 3 * 7], rest[3 * 7 :]
    sems, rest = rest[: 5 * 7], rest[5 * 7 :]
    s_n, r_n, s_rs, r_rs, s_small, r_small, s_small2, r_small2 = rest
    sources = (
        (lambda w: dkv_ref.at[w], True),
        (lambda w: ggu_hbm.at[0, tile(w, 128), :], True),
        (lambda w: ggu_hbm.at[1, tile(w, 128), :], True),
        (lambda w: gdown_hbm.at[:, tile(w, 128)], True),
        (lambda w: gout_hbm.at[:, tile(w, 128)], True),
        (lambda w: gq.at[tile(w, 128), :], True),
        (lambda w: gkv.at[tile(w, 128), :], True),
    )
    items = [
        Item(source, loaded, *buffers[3 * i : 3 * i + 3], sems[5 * i : 5 * i + 5])
        for i, (source, loaded) in enumerate(sources)
    ]
    pair, gate, up, down, out, query, keyval = items
    me = lax.axis_index("narrow")
    wide_me = lax.axis_index("wide")
    chip, core = wide_place()
    peer = [(wide_me, lax.rem(me + step, peers)) for step in range(1, peers)]
    mate = (2 * chip + 1 - core, me)
    across = [(2 * lax.rem(chip + step, chips) + core, me) for step in range(1, chips)]
    rows = tok_ref.shape[0]
    width = tok_ref.shape[1]
    mine = pl.ds(pl.multiple_of(me * rows, rows), rows)
    span = 256

    def remote(src, dst, ssem, rsem, there):
        return pltpu.make_async_remote_copy(
            src_ref=src, dst_ref=dst, send_sem=ssem, recv_sem=rsem,
            device_id=there, device_id_type=MESH,
        )

    def spread(ref, phase):
        copies = [
            remote(ref.at[mine, :], ref.at[mine, :], s_n.at[phase, i], r_n.at[phase, i], peer[i])
            for i in range(peers - 1)
        ]
        for copy in copies:
            copy.start()
        return copies

    greet(peer + across + [mate])
    stage_one(pair, chips)
    layer_ref[mine, :] = rows_ref[...]
    layer_copies = spread(layer_ref, 0)

    def grad_query(j, carry):
        gq[tile(j, span), :] = dot_tn(n1_ref[:, tile(j, span)], dq_ref[...]).astype(bf16)
        return carry

    stage_two(pair, chips)
    for item in (gate, up, down, out):
        stage_one(item, chips)
    lax.fori_loop(0, width // span, grad_query, 0)
    stage_one(query, chips)
    arrive(pair, chips)
    total = block_total(pair, pl.ds(0, dkv.shape[0]), chips)
    lane = lax.broadcasted_iota(jnp.int32, total.shape, 1)
    turned = total * cos_ref[...] - swap_halves(total) * sin_ref[...]
    dkv[...] = jnp.where(lane < HD, turned, total).astype(bf16)

    chunk = width // chunks

    def rs_copy(slot, c):
        theirs = pl.ds(pl.multiple_of(peer[slot][1] * rows, rows), rows)
        return remote(
            send.at[theirs, tile(c, chunk)], recv.at[slot, :, tile(c, chunk)],
            s_rs.at[slot, c], r_rs.at[slot, c], peer[slot],
        )

    def scatter(c, carry):
        columns = tile(c, chunk)
        send[:, columns] = (
            dot_nt(dq_ref[...], wq_ref[columns, :]) + dot_nt(dkv[...], wkv_ref[columns, :])
        ).astype(bf16)
        for slot in range(peers - 1):
            rs_copy(slot, c).start()
        return carry

    lax.fori_loop(0, chunks, scatter, 0)

    def grad_keyval(j, carry):
        gkv[tile(j, span), :] = dot_tn(n1_ref[:, tile(j, span)], dkv[...]).astype(bf16)
        return carry

    lax.fori_loop(0, width // span, grad_keyval, 0)
    stage_one(keyval, chips)
    for item in (gate, up):
        stage_two(item, chips)

    def scatter_wait(c, carry):
        for slot in range(peers - 1):
            rs_copy(slot, c).wait()
        return carry

    lax.fori_loop(0, chunks, scatter_wait, 0)
    total = send[mine, :].astype(f32)
    for slot in range(peers - 1):
        total = total + recv[slot].astype(f32)
    values = tok_ref[...].astype(f32)
    inverse = lax.rsqrt(jnp.mean(values * values, axis=-1, keepdims=True) + norm_eps)
    z1 = values * inverse
    gain_part[...] = jnp.where(
        lax.broadcasted_iota(jnp.int32, gain_part.shape, 0) == 0,
        jnp.sum(total * z1, axis=0, keepdims=True), gain2_ref[...],
    )
    gain_copy = remote(gain_part, gain_mate, s_small.at[0], r_small.at[0], mate)
    gain_copy.start()
    weighted = total * gains_ref[0:1, :].astype(f32)
    grad_ref[mine, :] = (
        dh_ref[...] + inverse * (weighted - z1 * jnp.mean(weighted * z1, axis=-1, keepdims=True))
    ).astype(bf16)
    grad_copies = spread(grad_ref, 1)

    for item in (down, out, query, keyval):
        stage_two(item, chips)
    gain_copy.wait()
    gain_mate[...] = gain_mate[...] + gain_part[...]
    gain_copies = []
    for step in range(chips - 1):
        there = across[step][0]
        copy = remote(
            gain_mate.at[:, tile(there, 128)], gain_in.at[step],
            s_small.at[step + 1], r_small.at[step + 1], across[step],
        )
        copy.start()
        gain_copies.append(copy)
    squares = jnp.zeros((1, 1), f32)
    for item, share in (
        (gate, gu_ref.at[0]), (up, gu_ref.at[1]), (down, down_ref), (out, out_ref),
        (query, q_ref), (keyval, kv_ref),
    ):
        arrive(item, chips)
        squares = squares + finish(item, share, chips)
    for copy in gain_copies:
        copy.wait()
    total = gain_mate[:, tile(wide_me, 128)]
    for step in range(chips - 1):
        total = total + gain_in[step]
    row = lax.broadcasted_iota(jnp.int32, total.shape, 0)
    gain_near[peers - 1] = jnp.where(row < 2, total, jnp.broadcast_to(squares, total.shape))
    near_copies = [
        remote(gain_near.at[peers - 1], gain_near.at[i], s_n.at[2, i], r_n.at[2, i], peer[i])
        for i in range(peers - 1)
    ]
    for copy in near_copies:
        copy.start()
    for copy in near_copies:
        copy.wait()
    total = gain_near[0]
    for i in range(1, peers):
        total = total + gain_near[i]
    gains_out_ref[...] = total
    kept = jnp.where(row < 2, total, 0.0)
    gain_squares = jnp.sum(jnp.sum(kept * kept, axis=1, keepdims=True), axis=0, keepdims=True)
    norm_own[...] = total[2:3, :] + jnp.broadcast_to(gain_squares, norm_own.shape)
    copy = remote(norm_own, norm_mate, s_small2.at[0], r_small2.at[0], mate)
    copy.start()
    copy.wait()
    norm_mate[...] = norm_mate[...] + norm_own[...]
    copies = [
        remote(norm_mate, norm_in.at[step], s_small2.at[step + 1], r_small2.at[step + 1], across[step])
        for step in range(chips - 1)
    ]
    for copy in copies:
        copy.start()
    for copy in copies:
        copy.wait()
    total = norm_mate[...]
    for step in range(chips - 1):
        total = total + norm_in[step]
    norm_ref[...] = jnp.sqrt(total)
    for copy in layer_copies + grad_copies:
        copy.wait()
    for item in items:
        drain(item, chips)


def last(
    peers, chips, dkv, dq, n1, tok_rows, gains, wq, wkv, dh, layer_rows, gain2, cosine, sine,
    gout, ggu, gdown,
):
    count, width = n1.shape
    rows = tok_rows.shape[0]
    wide_count = 2 * chips
    share = width // wide_count
    units = gdown.shape[0]
    heads = gout.shape[0]
    chunks = 4
    here = pl.BlockSpec(memory_space=pltpu.VMEM)
    anywhere = pl.BlockSpec(memory_space=pl.ANY)
    shape = jax.ShapeDtypeStruct
    dma = pltpu.SemaphoreType.DMA
    blocks = (
        (count, 2 * HD), (share, units), (share, units), (units, share), (heads, share),
        (share, heads), (share, 2 * HD),
    )
    buffers, sems = [], []
    for block in blocks:
        buffers += [
            pltpu.VMEM((chips, *block), bf16), pltpu.VMEM((chips, *block), bf16),
            pltpu.VMEM((chips - 1, *block), bf16),
        ]
        sems += [dma((chips,)), dma((chips,)), dma((chips - 1,)), dma((chips - 1,)), dma((chips,))]
    return pl.pallas_call(
        functools.partial(last_kernel, peers, chips, chunks),
        out_shape=(
            shape((count, width), bf16),
            shape((count, width), bf16),
            shape((share, heads), f32),
            shape((share, 2 * HD), f32),
            shape((heads, share), f32),
            shape((2, share, units), f32),
            shape((units, share), f32),
            shape((8, share), f32),
            shape((8, share), f32),
        ),
        in_specs=[here] * 12 + [anywhere] * 3,
        out_specs=(here,) * 9,
        scratch_shapes=[
            pltpu.VMEM((count, 2 * HD), bf16),
            pltpu.VMEM((width, heads), bf16),
            pltpu.VMEM((width, 2 * HD), bf16),
            pltpu.VMEM((count, width), bf16),
            pltpu.VMEM((peers - 1, rows, width), bf16),
            pltpu.VMEM((8, width), f32),
            pltpu.VMEM((8, width), f32),
            pltpu.VMEM((chips - 1, 8, share), f32),
            pltpu.VMEM((peers, 8, share), f32),
            pltpu.VMEM((8, share), f32),
            pltpu.VMEM((8, share), f32),
            pltpu.VMEM((chips - 1, 8, share), f32),
            *buffers,
            *sems,
            dma((3, peers - 1)),
            dma((3, peers - 1)),
            dma((peers - 1, chunks)),
            dma((peers - 1, chunks)),
            dma((chips,)),
            dma((chips,)),
            dma((chips,)),
            dma((chips,)),
        ],
        compiler_params=pltpu.CompilerParams(
            collective_id=3, has_side_effects=True, vmem_limit_bytes=63 * MB
        ),
        name="last",
    )(
        dkv, dq, n1, tok_rows, gains, wq, wkv, dh, layer_rows, gain2, cosine, sine, gout, ggu, gdown
    )


def rope_tables(positions, head_width):
    half_width = head_width // 2
    exponent = jnp.arange(half_width, dtype=jnp.float32) * (2.0 / head_width)
    base_freq = jnp.power(jnp.float32(rope_theta), -exponent)
    wavelen = 2.0 * math.pi / base_freq
    smooth = (rope_context / wavelen - rope_low) / (rope_high - rope_low)
    blended = (1.0 - smooth) * base_freq / rope_factor + smooth * base_freq
    scaled = jnp.where(
        wavelen < rope_context / rope_high,
        base_freq,
        jnp.where(wavelen > rope_context / rope_low, base_freq / rope_factor, blended),
    )
    angles = positions.astype(jnp.float32)[:, None] * scaled[None, :]
    return (jnp.cos(angles), jnp.sin(angles))


def adam_update(weight, gradient, old_first, old_second, step_rate, decay_factor):
    momentum = beta_first * old_first + (1.0 - beta_first) * gradient
    variance = beta_second * old_second + (1.0 - beta_second) * gradient * gradient
    corrected = momentum / (1.0 - beta_first**STEP)
    second_hat = variance / (1.0 - beta_second**STEP)
    updated = weight * (1.0 - step_rate * decay_factor) - step_rate * corrected / (
        jnp.sqrt(second_hat) + adam_eps
    )
    return (updated, momentum, variance)


def shards(
    tokens,
    cotangent,
    lengths,
    query_weight,
    keyval_weight,
    output_weight,
    gateup_weight,
    down_weight,
    norm_gains,
    query_first,
    keyval_first,
    output_first,
    gateup_first,
    down_first,
    gains_first,
    query_second,
    keyval_second,
    output_second,
    gateup_second,
    down_second,
    gains_second,
):
    bucket_count, row_count, model_width = tokens.shape
    wide_count = lax.axis_size("wide")
    narrow_count = lax.axis_size("narrow")
    wide_rank = lax.axis_index("wide")
    narrow_rank = lax.axis_index("narrow")
    token_count = bucket_count * row_count
    share_rows = token_count // narrow_count
    positions = wide_rank * row_count + jnp.arange(row_count, dtype=jnp.int32)
    cosine, sine_table = rope_tables(positions, HD)
    cosine = jnp.tile(jnp.concatenate([cosine, cosine], axis=1), (bucket_count, 2))
    sine_table = jnp.tile(jnp.concatenate([-sine_table, sine_table], axis=1), (bucket_count, 2))
    inputs = tokens.reshape(token_count, model_width)
    live_mask = (positions[None, :] < lengths[:, None]).astype(jnp.bfloat16)
    grad_low = (cotangent * live_mask[:, :, None]).reshape(token_count, model_width)
    pair_weight = jnp.concatenate([keyval_weight[0], keyval_weight[1]], axis=1)

    def rows_of(values):
        return lax.dynamic_slice_in_dim(values, narrow_rank * share_rows, share_rows, 0)

    normed_one, queries, pairs = front(
        wide_count, inputs, norm_gains, query_weight, pair_weight, cosine, sine_table
    )
    attended_low, attended, logs = attend(lengths, queries, pairs)
    (
        hidden, result_rows, grad_heads, grad_hidden, gain_two, output_grad, gateup_grad, down_grad,
    ) = middle(
        narrow_count, attended_low, output_weight, rows_of(inputs),
        rows_of(grad_low), grad_low, norm_gains, gateup_weight, down_weight,
    )
    grad_query, grad_pairs = attend_back(
        lengths, queries, pairs, attended, logs, grad_heads, cosine, sine_table
    )
    (
        layer_out, input_grad, query_sum, pair_sum, output_sum, gateup_sum, down_sum, gains_sum, norm,
    ) = last(
        narrow_count, wide_count // 2, grad_pairs, grad_query, normed_one, rows_of(inputs),
        norm_gains, query_weight, pair_weight, grad_hidden, result_rows, gain_two, cosine,
        sine_table, output_grad, gateup_grad, down_grad,
    )
    layer_out = layer_out.reshape(bucket_count, row_count, model_width)
    input_grad = input_grad.reshape(bucket_count, row_count, model_width)
    keyval_sum = jnp.stack([pair_sum[:, :HD], pair_sum[:, HD:]])
    gains_sum = gains_sum[:2]
    reduced = (query_sum, keyval_sum, output_sum, gateup_sum, down_sum, gains_sum)
    grad_norm = norm[0, 0]
    factor = jnp.minimum(1.0, clip_limit / (grad_norm + 1e-06))

    def owned(weight, along):
        piece_size = weight.shape[along] // wide_count
        return lax.dynamic_slice_in_dim(weight, wide_rank * piece_size, piece_size, along).astype(
            jnp.float32
        )

    olds = (
        owned(query_weight, 0),
        owned(keyval_weight, 1),
        owned(output_weight, 1),
        owned(gateup_weight, 1),
        owned(down_weight, 1),
        owned(norm_gains, 1),
    )
    firsts = (query_first, keyval_first, output_first, gateup_first, down_first, gains_first)
    seconds = (query_second, keyval_second, output_second, gateup_second, down_second, gains_second)
    clipped = tuple((matrix * factor for matrix in reduced))
    results = []
    for number in range(6):
        step_rate = gain_rate if number == 5 else learn_rate
        decay_factor = 0.0 if number == 5 else decay_rate
        results.append(
            adam_update(
                olds[number],
                clipped[number],
                firsts[number],
                seconds[number],
                step_rate,
                decay_factor,
            )
        )
    return (
        layer_out,
        input_grad,
        clipped[0],
        clipped[1],
        clipped[2],
        clipped[3],
        clipped[4],
        clipped[5],
        grad_norm,
        results[0][1],
        results[1][1],
        results[2][1],
        results[3][1],
        results[4][1],
        results[5][1],
        results[0][2],
        results[1][2],
        results[2][2],
        results[3][2],
        results[4][2],
        results[5][2],
        results[0][0],
        results[1][0],
        results[2][0],
        results[3][0],
        results[4][0],
        results[5][0],
    )


def solution(mesh):
    return jax.shard_map(
        shards,
        mesh=mesh,
        in_specs=(
            P(None, "wide", None),
            P(None, "wide", None),
            P(),
            P(None, "narrow"),
            P(None, None, "narrow"),
            P("narrow", None),
            P(None, None, "narrow"),
            P("narrow", None),
            P(),
            P("wide", "narrow"),
            P(None, "wide", "narrow"),
            P("narrow", "wide"),
            P(None, "wide", "narrow"),
            P("narrow", "wide"),
            P(None, "wide"),
            P("wide", "narrow"),
            P(None, "wide", "narrow"),
            P("narrow", "wide"),
            P(None, "wide", "narrow"),
            P("narrow", "wide"),
            P(None, "wide"),
        ),
        out_specs=(
            P(None, "wide", None),
            P(None, "wide", None),
            P("wide", "narrow"),
            P(None, "wide", "narrow"),
            P("narrow", "wide"),
            P(None, "wide", "narrow"),
            P("narrow", "wide"),
            P(None, "wide"),
            P(),
            P("wide", "narrow"),
            P(None, "wide", "narrow"),
            P("narrow", "wide"),
            P(None, "wide", "narrow"),
            P("narrow", "wide"),
            P(None, "wide"),
            P("wide", "narrow"),
            P(None, "wide", "narrow"),
            P("narrow", "wide"),
            P(None, "wide", "narrow"),
            P("narrow", "wide"),
            P(None, "wide"),
            P("wide", "narrow"),
            P(None, "wide", "narrow"),
            P("narrow", "wide"),
            P(None, "wide", "narrow"),
            P("narrow", "wide"),
            P(None, "wide"),
        ),
        check_vma=False,
    )
```

time: 1020 us -> 455 us (0.45); the launches traced: 1010 us -> 456 us
  waiting for transfers between devices: 528 us -> 0 us
  Pallas kernels: 0 us -> 415 us
  blocking collectives: 165 us -> 0 us
  local copies, waits for them, and re-layouts: 121 us -> 24.8 us
  matrix products: 76.9 us -> 0 us
  starting transfers between devices: 39.9 us -> 0 us
  other arithmetic: 43 us -> 13.6 us
  between operations: 21.5 us -> 1.8 us
  loops' own time: 11.3 us -> 0 us
    pallas_call x0 -> x5, Pallas kernels: none -> 415 us  [the longest x1 228 us: last(): pl.pallas_call(functools.partial(last_kernel, peers, chips, chunks), out_...]
    reduce_scatter x5 -> x0, waiting for transfers between devices: 314 us -> none  [the longest x4 196 us: row_sum(): lax.psum_scatter(values.astype(jnp.bfloat16), 'narrow', scatter_dimension...]
    unnamed x12 -> x0, waiting for transfers between devices: 120 us -> none
    psum x2 -> x0, blocking collectives: 104 us -> none  [the longest x1 68.2 us: shards(): total_squares = lax.psum(local_squares, ('wide', 'narrow'))]
    dot_general x21 -> x0, matrix products: 76.1 us -> none  [the longest x1 9.09 us: shards(): jnp.einsum('cnf,cdf->nd', grad_gateup, gateup_weight, preferred_element_t...]
    unnamed x137 -> x83, local copies, waits for them, and re-layouts: 82.9 us -> 19.7 us
    all_to_all x6 -> x0, waiting for transfers between devices: 61.3 us -> none  [the longest x3 46.9 us: sent_to_all(): lax.all_to_all(jnp.broadcast_to(x[None], (peers, *x.shape)), axis, 0, 0,...]
    all_to_all x6 -> x0, starting transfers between devices: 38.7 us -> none  [the longest x3 25.9 us: sent_and_summed(): blocks = lax.all_to_all(cut_along(x, dim, peers), axis, 0, 0, tiled=True)]
  transfers between devices with their start and end apart: 15 -> 0, of which waited for: 11 -> 0; matrix products, arithmetic and copies ran while one was open for 11% -> 0% of each run, Pallas kernels for 0% -> 0%
where the time goes in v1:
time: 455 us; the launch traced here: 456 us
  Pallas kernels  415 us (91%)
  local copies, waits for them, and re-layouts  24.8 us (5%)
  other arithmetic  13.6 us (3%)
    pallas_call x1, Pallas kernels, last(): pl.pallas_call(functools.partial(last_kernel, peers, chips, chunks), out_...  228 us
    pallas_call x1, Pallas kernels, middle(): pl.pallas_call(functools.partial(middle_kernel, peers, chunks), out_shape...  150 us
    pallas_call x1, Pallas kernels, front(): pl.pallas_call(functools.partial(front_kernel, others), out_shape=(shape(...  24.8 us
    unnamed x83, local copies, waits for them, and re-layouts  19.7 us
    sub x6, other arithmetic, adam_update(): weight * (1.0 - step_rate * decay_factor)  11.2 us

profile of v1, /device:TPU:1, one launch (start us, length us, event | category | flops | bytes accessed | tf_op | source)
XLA Modules:
  0.0 455.7 jit_solution(18319278385388736344)
XLA Ops:
  3.0 24.8 %front.1 = (bf16[512,2048]{1,0:T(8,128)(2,1)S(1)}, bf16[512,256]{1,0:T(8,128)(2,1)S(1)}, bf16[16,512,128]{2,1,0:T(8,128)(2,1)}) custom-call(bf16[512,2048]{1,0:T(8,128)(2,1)} %bitcast.23, bf16[2,2048]{1,0:T(2,128)(2,1)S(1)} %copy-done.16, bf16[2048,256]{1,0:T(8,128)(2,1)S(1)} %copy-done.3, bf16[2048,128]{1,0:T(8,128)(2,1)S(1)} %pad_maximum_fusion.wkv_ref, ...), custom_call_target="tpu_custom_call" | custom-call | tf_op jit(solution)/shard_map/front/pallas_call | solution.py:401
  27.9 1.3 copy-done.7
  29.2 1.7 copy-done
  30.9 5.6 %attend.1 = (bf16[512,256]{1,0:T(8,128)(2,1)S(1)}, f32[512,256]{1,0:T(8,128)S(1)}, f32[8,256]{1,0:T(8,128)S(1)}) custom-call(s32[2]{0:T(128)S(1)} %copy-done.17, bf16[512,256]{1,0:T(8,128)(2,1)S(1)} %get-tuple-element.51.q_ref, bf16[16,512,128]{2,1,0:T(8,128)(2,1)S(1)} %copy-done), custom_call_target="tpu_custom_call" | custom-call | tf_op jit(solution)/shard_map/attend/pallas_call | solution.py:490
  38.0 1.8 broadcast_multiply_fusion
  39.9 0.8 constant_dynamic-slice_fusion.2.dy_ref
  41.3 1.7 constant_dynamic-slice_fusion.3.tok_ref
  42.9 150.2 %middle.1 = (f32[64,2048]{1,0:T(8,128)}, bf16[64,2048]{1,0:T(8,128)(2,1)}, bf16[512,256]{1,0:T(8,128)(2,1)}, f32[64,2048]{1,0:T(8,128)}, f32[8,2048]{1,0:T(8,128...) custom-call(bf16[512,256]{1,0:T(8,128)(2,1)} %copy-done.13, ...), custom_call_target="tpu_custom_call" | custom-call | tf_op jit(solution)/shard_map/middle/pallas_call | solution.py:281
  193.2 1.6 copy-done.1
  194.8 1.0 copy-done.12
  195.8 0.9 copy-done.15
  196.8 6.6 %attend_back.1 = (bf16[512,256]{1,0:T(8,128)(2,1)S(1)}, bf16[16,512,128]{2,1,0:T(8,128)(2,1)S(1)}) custom-call(s32[2]{0:T(128)S(1)} %copy-done.17, bf16[512,256]{1,0:T(8,128)(2,1)S(1)} %copy-done.10, bf16[16,512,128]{2,1,0:T(8,128)(2,1)S(1)} %copy-done.1, f32[512,256]{1,0:T(8,128)S(1)} %copy-done.12, f32[8,256]{1,0:T(8,128)S(1)} %get-tuple-element.54.log_ref, ...), custom_call_target="tpu_custom_call" | custom-call | tf_op jit(solution)/shard_map/attend_back/pallas_call | solution.py:569
  203.4 1.3 copy-done.8
  205.4 228.3 %last.1 = (bf16[512,2048]{1,0:T(8,128)(2,1)}, bf16[512,2048]{1,0:T(8,128)(2,1)}, f32[128,256]{1,0:T(8,128)}, f32[128,128]{1,0:T(8,128)}, f32[256,128]{1,0:T(8,12...) custom-call(bf16[16,512,128]{2,1,0:T(8,128)(2,1)} %copy-done.8, ...), custom_call_target="tpu_custom_call" | custom-call | tf_op jit(solution)/shard_map/last/pallas_call | solution.py:909
  433.7 1.3 slice.20
  435.8 1.3 divide_subtract_fusion.5
  437.1 2.9 divide_subtract_fusion.1
  440.0 3.5 divide_subtract_fusion
  443.5 1.8 divide_subtract_fusion.2
  446.4 0.9 copy.82
  450.3 1.7 divide_subtract_fusion.4
  452.0 1.3 copy.95
  453.3 1.0 copy-done.19
  454.4 1.3 copy.96
  (88 shorter events, 9.2 us)
Async XLA Ops:
  1.2 192.0 %copy-start.4 = (f32[512,128]{1,0:T(8,128)}, f32[512,128]{1,0:T(8,128)S(1)}, u32[]{:S(2)}) copy-start(f32[512,128]{1,0:T(8,128)S(1)} %copy.75.sin_ref) | copy-start | bytes 786436
  2.6 25.2 %copy-start.2 = (bf16[2048,128]{1,0:T(8,128)(2,1)}, bf16[2048,128]{1,0:T(8,128)(2,1)S(1)}, u32[]{:S(2)}) copy-start(bf16[2048,128]{1,0:T(8,128)(2,1)S(1)} %pad_maximum_fusion.wkv_ref) | copy-start | bytes 1572868
  3.0 26.1 %copy-start.17 = (s32[2]{0:T(128)S(1)}, s32[2]{0:T(128)}, u32[]{:S(2)}) copy-start(s32[2]{0:T(128)} %len_ref.3) | copy-start | bytes 28
  29.2 10.7 %copy-start.9 = (bf16[512,256]{1,0:T(8,128)(2,1)}, bf16[512,256]{1,0:T(8,128)(2,1)S(1)}, u32[]{:S(2)}) copy-start(bf16[512,256]{1,0:T(8,128)(2,1)S(1)} %get-tuple-element.51.q_ref) | copy-start | bytes 786436
  29.2 1.7 copy-start
  39.8 1.4 copy-start.18
  42.9 150.2 %copy-start.6 = (f32[512,128]{1,0:T(8,128)S(1)}, f32[512,128]{1,0:T(8,128)}, u32[]{:S(2)}) copy-start(f32[512,128]{1,0:T(8,128)} %copy-done.5) | copy-start | bytes 786436
  42.9 150.2 %copy-start.10 = (bf16[512,256]{1,0:T(8,128)(2,1)S(1)}, bf16[512,256]{1,0:T(8,128)(2,1)}, u32[]{:S(2)}) copy-start(bf16[512,256]{1,0:T(8,128)(2,1)} %copy-done.9) | copy-start | bytes 786436
  193.2 1.6 copy-start.1
  205.4 230.4 %copy-start.33 = (f32[2,128]{1,0:T(2,128)S(1)}, f32[2,128]{1,0:T(2,128)}, u32[]{:S(2)}) copy-start(f32[2,128]{1,0:T(2,128)} %param.41) | copy-start | bytes 3076
  205.4 230.4 %copy-start.34 = (f32[2,128]{1,0:T(2,128)S(1)}, f32[2,128]{1,0:T(2,128)}, u32[]{:S(2)}) copy-start(f32[2,128]{1,0:T(2,128)} %param.35) | copy-start | bytes 3076
  433.7 6.2 %copy-start.21 = (f32[2,128,1024]{2,1,0:T(8,128)S(1)}, f32[2,128,1024]{2,1,0:T(8,128)}, u32[]{:S(2)}) copy-start(f32[2,128,1024]{2,1,0:T(8,128)} %param.39) | copy-start | bytes 3145732
  433.7 6.2 %copy-start.22 = (f32[2,128,1024]{2,1,0:T(8,128)S(1)}, f32[2,128,1024]{2,1,0:T(8,128)}, u32[]{:S(2)}) copy-start(f32[2,128,1024]{2,1,0:T(8,128)} %param.33) | copy-start | bytes 3145732
  433.7 6.2 %copy-start.23 = (f32[2,128,1024]{2,1,0:T(8,128)S(1)}, f32[2,128,1024]{2,1,0:T(8,128)}, u32[]{:S(2)}) copy-start(f32[2,128,1024]{2,1,0:T(8,128)} %get-tuple-element.72) | copy-start | bytes 3145732
  439.9 3.5 copy-start.26
  440.0 3.5 copy-start.27
  440.0 3.5 copy-start.31
  440.0 5.4 %copy-start.25 = (f32[128,128]{1,0:T(8,128)S(1)}, f32[128,128]{1,0:T(8,128)}, u32[]{:S(2)}) copy-start(f32[128,128]{1,0:T(8,128)} %get-tuple-element.70) | copy-start | bytes 196612
  440.0 6.3 %copy-start.32 = (f32[2,128,64]{1,2,0:T(8,128)S(1)}, f32[2,128,64]{1,2,0:T(8,128)}, u32[]{:S(2)}) copy-start(f32[2,128,64]{1,2,0:T(8,128)} %param.31) | copy-start | bytes 196612
  443.5 6.9 %copy-start.28 = (f32[128,256]{1,0:T(8,128)S(1)}, f32[128,256]{1,0:T(8,128)}, u32[]{:S(2)}) copy-start(f32[128,256]{1,0:T(8,128)} %param.36) | copy-start | bytes 393220
  443.5 6.9 %copy-start.29 = (f32[128,256]{1,0:T(8,128)S(1)}, f32[128,256]{1,0:T(8,128)}, u32[]{:S(2)}) copy-start(f32[128,256]{1,0:T(8,128)} %param.30) | copy-start | bytes 393220
  443.5 6.9 %copy-start.30 = (f32[128,256]{1,0:T(8,128)S(1)}, f32[128,256]{1,0:T(8,128)}, u32[]{:S(2)}) copy-start(f32[128,256]{1,0:T(8,128)} %get-tuple-element.68) | copy-start | bytes 393220
  443.5 8.5 %copy-start.20 = (bf16[512,2048]{1,0:T(8,128)(2,1)S(1)}, bf16[512,2048]{1,0:T(8,128)(2,1)}, u32[]{:S(2)}) copy-start(bf16[512,2048]{1,0:T(8,128)(2,1)} %get-tuple-element.66) | copy-start | bytes 6291460
  452.0 2.3 copy-start.19
  (11 other events, 11.4 us)
